TPU v7x, 32 devices: a whole 2x2x4 slice. The times are simulated.
32 devices in a mesh: section: 2 (over x), dp: 4 (over z), tensor: 4 (over y, core).
Axes of the slice: x: 2, y: 2, z: 4, core: 2. Of those that a mesh axis runs over, the one named last changes fastest.
Arguments:
- hidden: bfloat16 [8, 1024, 768], P('dp', 'tensor'), may hold values from -6 to 6
- cotangent: bfloat16 [8, 1024, 768], P('dp', 'tensor'), may hold values from -6 to 6
- pair_lengths: int32 [8], P('dp'), may hold values from 256 to 1024, as said below
- query_lengths: int32 [8], P('dp'), may hold values from 1 to 256, as said below
- buckets: int32 [2047], replicated, may hold values from 0 to 31
- qkv_weight: bfloat16 [2, 768, 3, 768], P('section', None, None, 'tensor'), may hold values from -0.21875 to 0.21875
- qv_bias: float32 [2, 2, 768], P('section', None, 'tensor'), may hold values from -3 to 3
- out_weight: bfloat16 [2, 768, 768], P('section', 'tensor'), may hold values from -1.25 to 1.25
- up_weight: bfloat16 [2, 768, 3072], P('section', None, 'tensor'), may hold values from -0.21875 to 0.21875
- ffn_bias: float32 [2, 3072], P('section', 'tensor'), may hold values from -3 to 3
- down_weight: bfloat16 [2, 3072, 768], P('section', 'tensor'), may hold values from -0.109375 to 0.109375
- norm_gains: float32 [2, 2, 768], P('section'), may hold values from 0.5 to 1.5
- vectors: float32 [2, 4, 768], P('section'), may hold values from -3 to 3
- bias_table: float32 [2, 12, 64], P('section', 'tensor'), may hold values from -5 to 5
Outputs:
- edges: float32 [2, 8, 1024, 768], P('section', 'dp', 'tensor')
- qkv_weight_grad: float32 [2, 768, 3, 768], P('section', None, None, 'tensor')
- qv_bias_grad: float32 [2, 2, 768], P('section', None, 'tensor')
- out_weight_grad: float32 [2, 768, 768], P('section', 'tensor')
- up_weight_grad: float32 [2, 768, 3072], P('section', None, 'tensor')
- ffn_bias_grad: float32 [2, 3072], P('section', 'tensor')
- down_weight_grad: float32 [2, 3072, 768], P('section', 'tensor')
- gain_grad: float32 [2, 2, 768], P('section', None, 'tensor')
- vector_grad: float32 [2, 4, 768], P('section', None, 'tensor')
- table_grad: float32 [2, 12, 64], P('section', 'tensor')
Inputs may be any that keep to these rules, and one draw needn't show every extreme that they name: `pair_lengths`: in each group of 2 consecutive pairs one, drawn from the seed, has all 1024 tokens live. `query_lengths`: A query is never longer than the shortest pair.
All inputs are finite; a program needn't handle non-finite values.
Results may differ from a plain program's by a relative error of at most 0.019.
Values may be sent and summed in bfloat16 or wider, within the bound.
No kernel may reach another device: no remote copies, remote signals or barrier semaphores. Data moves between devices by JAX's collectives and lax.ppermute only.
A program may use at most 320 MiB of HBM per device.

v0:
```python
import functools

import jax
import jax.numpy as jnp
from jax import lax
from jax.experimental import pallas as pl
from jax.experimental.pallas import tpu as pltpu
from jax.sharding import PartitionSpec as P


f32 = jnp.float32
bf16 = jnp.bfloat16
EPS = 1e-05
HEAD = 64
NEG = -1e30
SWAP_Y = [(0, 2), (2, 0), (1, 3), (3, 1)]
SWAP_C = [(0, 1), (1, 0), (2, 3), (3, 2)]
NT = (((1,), (1,)), ((), ()))
TN = (((0,), (0,)), ((), ()))
NN = (((1,), (0,)), ((), ()))
KEY_BASE = (0, 512, 256, 768)
TILE_BASE = (0, 128, 512, 640)
STRIP = 1664
SPAN = STRIP + 128
PIECE = 32
MIB = 2**20
IN_VMEM = pl.BlockSpec(memory_space=pltpu.VMEM)


def cost(us, flops=0):
    return pl.CostEstimate(flops=flops, bytes_accessed=int(us * 3.4e6), transcendentals=0)


def dotf(a, b, dims=NN):
    return lax.dot_general(a, b, dims, preferred_element_type=f32)


def swap_y(value):
    return lax.ppermute(value, "tensor", SWAP_Y)


def swap_c(value):
    return lax.ppermute(value, "tensor", SWAP_C)


def make_strip(window_ref, h, kind, strip_ref):
    blocks = STRIP // 128
    lane = lax.broadcasted_iota(jnp.int32, (8, 128), 1)
    row = lax.broadcasted_iota(jnp.int32, (8, 128), 0)

    def rolled(first):
        at = 2 * h + kind
        seg = window_ref[at : at + 1, first : first + 128]
        seg = pltpu.roll(jnp.broadcast_to(seg, (8, 128)), 0, 1, stride=1, stride_axis=0)
        return [pltpu.roll(seg, 8 * q, 1) if q else seg for q in range(16)]

    high = rolled(128 * blocks)
    for a in range(blocks):
        low = rolled(128 * (blocks - 1 - a))
        for q in range(16):
            rows = slice(128 * a + 8 * q, 128 * a + 8 * q + 8)
            strip_ref[h, kind, rows, :] = jnp.where(lane >= row + 8 * q, high[q], low[q])
        high = low


def sum_strip(strip_ref, h, kind, held_ref):
    blocks = STRIP // 128
    lane = lax.broadcasted_iota(jnp.int32, (8, 128), 1)
    carry = jnp.zeros((8, 128), f32)
    for a in reversed(range(blocks)):
        low, high = jnp.zeros((8, 128), f32), jnp.zeros((8, 128), f32)
        for q in range(16):
            part = strip_ref[h, kind, 128 * a + 8 * q : 128 * a + 8 * q + 8, :]
            if q:
                part = pltpu.roll(part, 128 - 8 * q, 1)
            stays = lane < 128 - 8 * q
            high += jnp.where(stays, part, 0.0)
            low += jnp.where(stays, 0.0, part)
        first = 128 * (blocks - 1 - a)
        held_ref[0, h, kind, :, first : first + 128] = low + carry
        carry = high
    held_ref[0, h, kind, :, 128 * blocks : 128 * blocks + 128] = carry


def lane_mask(rows, which):
    lane = lax.broadcasted_iota(jnp.int32, (rows, 128), 1)
    return (lane < HEAD) if which == 0 else (lane >= HEAD)


def cross_mask(info_ref, tile, first):
    key_low = first < 256
    row_low = tile < 2
    if not key_low and not row_low:
        return None
    qlen, core = info_ref[0], info_ref[1]
    shape = (PIECE, 128)
    if row_low:
        row = 256 * core + 128 * tile + lax.broadcasted_iota(jnp.int32, shape, 1)
        row_side = row < qlen
    if key_low:
        key_side = first + lax.broadcasted_iota(jnp.int32, shape, 0) < qlen
    if row_low and key_low:
        return row_side != key_side
    return row_side if row_low else key_side


def pieces(kb):
    for at in range(0, 256, PIECE):
        yield KEY_BASE[kb] + at, slice(256 * kb + at, 256 * kb + at + PIECE), slice(at, at + PIECE)


def strip_rows(tile, first):
    start = first - TILE_BASE[tile] + 640
    return slice(start, start + PIECE)


def piece_scores(info_ref, raw, strip_ref, h, ib, first):
    parts = []
    for u in (0, 1):
        tile = 2 * ib + u
        rows = strip_rows(tile, first)
        bias = strip_ref[h, 0, rows, :]
        cross = cross_mask(info_ref, tile, first)
        if cross is not None:
            bias = jnp.where(cross, strip_ref[h, 1, rows, :], bias)
        parts.append(raw[:, 128 * u : 128 * u + 128] + bias)
    scores = jnp.concatenate(parts, 1)
    if first >= 256:
        live = first + lax.broadcasted_iota(jnp.int32, (PIECE, 256), 0) < info_ref[2]
        scores = jnp.where(live, scores, NEG)
    return scores


def by_eight(value):
    return value.reshape(PIECE // 8, 8, 256)


def whole(core, own, other):
    return jnp.concatenate([jnp.where(core == 0, own, other), jnp.where(core == 0, other, own)], 0)


def forward_kernel(
    info_ref,
    q_ref,
    k_ref,
    v_ref,
    ko_ref,
    vo_ref,
    win_ref,
    o_ref,
    lse_ref,
    strip_ref,
    score_ref,
    prob_ref,
):
    core = info_ref[1]
    for h in range(2):
        for kind in range(2):
            make_strip(win_ref, h, kind, strip_ref)
    keys = whole(core, k_ref[...], ko_ref[...])
    values = whole(core, v_ref[...], vo_ref[...])
    one = jnp.ones_like(values)
    turned = [jnp.where(lane_mask(1024, h), values, one).T for h in range(2)]
    for ib in range(2):
        rows = slice(256 * ib, 256 * ib + 256)
        query = q_ref[rows, :] * jnp.asarray(0.125, bf16)
        outs = []
        for h in range(2):
            one = jnp.where(lane_mask(256, h), query, jnp.zeros_like(query))
            top = None
            for kb in range(4):
                raw = dotf(keys[256 * kb : 256 * kb + 256], one, NT)
                for first, at, within in pieces(kb):
                    scores = piece_scores(info_ref, raw[within], strip_ref, h, ib, first)
                    score_ref[h, at, :] = scores
                    most = jnp.max(by_eight(scores), 0)
                    top = most if top is None else jnp.maximum(top, most)
            top = jnp.max(top, 0, keepdims=True)
            for kb in range(4):
                for _, at, _ in pieces(kb):
                    prob_ref[h, at, :] = jnp.exp(score_ref[h, at, :] - top).astype(bf16)
            mixed = dotf(turned[h], prob_ref[h])
            total = mixed[HEAD * (1 - h) : HEAD * (1 - h) + 1, :]
            lse_ref[0, h : h + 1, rows] = top + jnp.log(total)
            outs.append(mixed[HEAD * h : HEAD * h + HEAD, :] / total)
        o_ref[rows, :] = jnp.concatenate(outs, 0).T.astype(bf16)


def kv_blocks(groups, first=0):
    half = groups // 2
    return [
        pl.BlockSpec((512, 128), lambda i, s: (0, i + first)),
        pl.BlockSpec((512, 128), lambda i, s: (0, i + first + groups)),
        pl.BlockSpec((512, 128), lambda i, s: (0, (i + first + half) % groups)),
        pl.BlockSpec((512, 128), lambda i, s: (0, (i + first + half) % groups + groups)),
    ]


def attend_forward(info, q, kv, kv_other, window):
    groups = q.shape[1] // 128
    block = pl.BlockSpec((512, 128), lambda i, s: (0, i))
    return pl.pallas_call(
        forward_kernel,
        grid_spec=pltpu.PrefetchScalarGridSpec(
            num_scalar_prefetch=1,
            grid=(groups,),
            in_specs=[
                block,
                *kv_blocks(groups),
                pl.BlockSpec((8, SPAN), lambda i, s: (i, 0)),
            ],
            out_specs=[block, pl.BlockSpec((1, 2, 512), lambda i, s: (i, 0, 0))],
            scratch_shapes=[
                pltpu.VMEM((2, 2, STRIP, 128), f32),
                pltpu.VMEM((2, 1024, 256), f32),
                pltpu.VMEM((2, 1024, 256), bf16),
            ],
        ),
        out_shape=[
            jax.ShapeDtypeStruct((512, 128 * groups), bf16),
            jax.ShapeDtypeStruct((groups, 2, 512), f32),
        ],
        compiler_params=pltpu.CompilerParams(vmem_limit_bytes=24 * MIB),
        cost_estimate=cost(17),
        name="attend_forward",
    )(info, q, kv, kv, kv_other, kv_other, window)


def backward_kernel(with_table, *refs):
    info_ref, q_ref, k_ref, v_ref, ko_ref, vo_ref, do_ref, lse_ref, win_ref = refs[:9]
    dq_ref, dk_ref, dv_ref, dko_ref, dvo_ref, *rest = refs[9:]
    core = info_ref[1]
    *rest, strip_ref, wide_ref, term_ref, prob_ref, grad_ref = rest
    for h in range(2):
        for kind in range(2):
            make_strip(win_ref, h, kind, strip_ref)
    if with_table:
        held_ref, strip_grad_ref = rest
        strip_grad_ref[...] = jnp.zeros_like(strip_grad_ref)
    keys = whole(core, k_ref[...], ko_ref[...])
    values = whole(core, v_ref[...], vo_ref[...])
    keys_turned = keys.T
    key_grad = value_grad = 0.0
    for ib in range(2):
        rows = slice(256 * ib, 256 * ib + 256)
        query = q_ref[rows, :] * jnp.asarray(0.125, bf16)
        grad = do_ref[rows, :]
        query_grads = []
        for h in range(2):
            mask = lane_mask(256, h)
            one = jnp.where(mask, query, jnp.zeros_like(query))
            grad_one = jnp.where(mask, grad, jnp.zeros_like(grad))
            log_total = lse_ref[0, h : h + 1, rows]
            row_term = 0.0
            for kb in range(4):
                kr = slice(256 * kb, 256 * kb + 256)
                raw = dotf(keys[kr], one, NT)
                grad_probs = dotf(values[kr], grad_one, NT)
                for first, at, within in pieces(kb):
                    scores = piece_scores(info_ref, raw[within], strip_ref, h, ib, first)
                    probs = jnp.exp(scores - log_total)
                    term = probs * grad_probs[within]
                    wide_ref[h, at, :] = probs
                    term_ref[h, at, :] = term
                    prob_ref[h, at, :] = probs.astype(bf16)
                    row_term = row_term + jnp.sum(by_eight(term), 0)
            row_term = jnp.sum(row_term, 0, keepdims=True)
            for kb in range(4):
                for first, at, _ in pieces(kb):
                    low = (term_ref[h, at, :] - wide_ref[h, at, :] * row_term).astype(bf16)
                    grad_ref[h, at, :] = low
                    if with_table:
                        for u in (0, 1):
                            tile = 2 * ib + u
                            where = strip_rows(tile, first)
                            part = low[:, 128 * u : 128 * u + 128].astype(f32)
                            strip_grad_ref[h, 0, where, :] += part
                            cross = cross_mask(info_ref, tile, first)
                            if cross is not None:
                                strip_grad_ref[h, 1, where, :] += jnp.where(cross, part, 0.0)
            value_grad = value_grad + dotf(prob_ref[h], grad_one)
            key_grad = key_grad + dotf(grad_ref[h], one)
            flat = dotf(keys_turned, grad_ref[h])
            query_grads.append(flat[HEAD * h : HEAD * h + HEAD, :])
        dq_ref[rows, :] = (jnp.concatenate(query_grads, 0).T * 0.125).astype(bf16)
    for grads, own_ref, other_ref in (
        (key_grad, dk_ref, dko_ref),
        (value_grad, dv_ref, dvo_ref),
    ):
        first, second = grads[:512], grads[512:]
        own_ref[...] = jnp.where(core == 0, first, second)
        other_ref[...] = jnp.where(core == 0, second, first).astype(bf16)
    if with_table:
        for h in range(2):
            for kind in range(2):
                sum_strip(strip_grad_ref, h, kind, held_ref)


def attend_backward(info, q, kv, kv_other, grad, lse, window, with_table, first, count):
    groups = q.shape[1] // 128
    block = pl.BlockSpec((512, 128), lambda i, s: (0, i + first))
    rows = lambda kind: jax.ShapeDtypeStruct((512, 128 * count), kind)
    out_specs = [pl.BlockSpec((512, 128), lambda i, s: (0, i))] * 5
    out_shape = [rows(bf16), rows(f32), rows(f32), rows(bf16), rows(bf16)]
    scratch = [pltpu.VMEM((2, 2, STRIP, 128), f32)]
    if with_table:
        out_specs.append(pl.BlockSpec((1, 2, 2, 8, SPAN), lambda i, s: (i, 0, 0, 0, 0)))
        out_shape.append(jax.ShapeDtypeStruct((count, 2, 2, 8, SPAN), f32))
        scratch = scratch * 2
    scratch += [pltpu.VMEM((2, 1024, 256), f32)] * 2 + [pltpu.VMEM((2, 1024, 256), bf16)] * 2
    return pl.pallas_call(
        functools.partial(backward_kernel, with_table),
        grid_spec=pltpu.PrefetchScalarGridSpec(
            num_scalar_prefetch=1,
            grid=(count,),
            in_specs=[
                block,
                *kv_blocks(groups, first),
                block,
                pl.BlockSpec((1, 2, 512), lambda i, s: (i + first, 0, 0)),
                pl.BlockSpec((8, SPAN), lambda i, s: (i + first, 0)),
            ],
            out_specs=out_specs,
            scratch_shapes=scratch,
        ),
        out_shape=out_shape,
        compiler_params=pltpu.CompilerParams(vmem_limit_bytes=36 * MIB),
        cost_estimate=cost(30),
        name="attend_backward",
    )(info, q, kv, kv, kv_other, kv_other, grad, lse, window)


def norm_parts(values):
    centre = jnp.mean(values, -1, keepdims=True)
    centred = values - centre
    scale = lax.rsqrt(jnp.mean(centred * centred, -1, keepdims=True) + EPS)
    return centred * scale, scale


def norm_back(grad, gain, normal, scale):
    scaled = grad * gain
    return scale * (
        scaled
        - jnp.mean(scaled, -1, keepdims=True)
        - normal * jnp.mean(scaled * normal, -1, keepdims=True)
    )


def normal_cdf(units):
    size = jnp.abs(units)
    t = 1.0 / (1.0 + (0.3275911 * 0.5**0.5) * size)
    bell = jnp.exp(-0.5 * units * units)
    poly = 0.5 * 1.061405429
    for coef in (-1.453152027, 1.421413741, -0.284496736, 0.254829592):
        poly = poly * t + 0.5 * coef
    tail = poly * t * bell
    return jnp.where(units >= 0, 1.0 - tail, tail), bell


def ffn_forward_kernel(
    keep,
    att_ref,
    x_ref,
    out_ref,
    up_ref,
    up_far_ref,
    down_ref,
    down_far_ref,
    bias_ref,
    gain_ref,
    shift_ref,
    result_ref,
    *rest,
):
    if keep:
        (
            low_ref,
            active_ref,
            slope_ref,
            n_one_ref,
            s_one_ref,
            n_two_ref,
            s_two_ref,
            normed_low,
            total,
        ) = rest
    else:
        normed_low, total = rest
    i = pl.program_id(0)

    @pl.when(i == 0)
    def _():
        before = x_ref[...].astype(f32) + (dotf(att_ref[...], out_ref[...]) + shift_ref[0:1, :])
        normal, scale = norm_parts(before)
        normed = normal * gain_ref[0:1, :] + shift_ref[1:2, :]
        normed_low[...] = normed.astype(bf16)
        total[...] = normed + shift_ref[2:3, :]
        if keep:
            n_one_ref[...] = normal
            s_one_ref[...] = scale
            low_ref[...] = normed_low[...]

    near = i < 2
    width = up_ref.shape[2]
    step = 256
    add = None
    for first in range(0, width, step):
        cols = slice(first, first + step)
        up = jnp.where(near, up_ref[0, :, cols], up_far_ref[0, :, cols])
        down = jnp.where(near, down_ref[0, cols, :], down_far_ref[0, cols, :])
        units = dotf(normed_low[...], up) + bias_ref[:, cols]
        side, bell = normal_cdf(units)
        active = (units * side).astype(bf16)
        if keep:
            active_ref[:, cols] = active
            slope_ref[:, cols] = (side + units * bell * 0.3989422804014327).astype(bf16)
        part = dotf(active, down)
        add = part if add is None else add + part
    total[...] += add

    @pl.when(i == pl.num_programs(0) - 1)
    def _():
        normal, scale = norm_parts(total[...])
        result = normal * gain_ref[1:2, :] + shift_ref[3:4, :]
        result_ref[...] = result.astype(result_ref.dtype)
        if keep:
            n_two_ref[...] = normal
            s_two_ref[...] = scale


def near_far(rows, cols):
    return [
        pl.BlockSpec((1, rows, cols), lambda i: (jnp.minimum(i, 1), 0, 0)),
        pl.BlockSpec((1, rows, cols), lambda i: (jnp.maximum(i - 2, 0), 0, 0)),
    ]


def ffn_forward(w, attended, inputs, keep, part=0, parts=1):
    rows, model = inputs.shape
    rows //= parts
    width = w["up"][0].shape[2]
    all_of = lambda *shape: pl.BlockSpec(shape, lambda i: (0,) * len(shape))
    by_step = pl.BlockSpec((rows, width), lambda i: (0, i))
    shape = lambda cols, kind: jax.ShapeDtypeStruct((rows, cols), kind)
    out_specs = [all_of(rows, model)]
    out_shape = [shape(model, f32 if keep else bf16)]
    if keep:
        out_specs += [all_of(rows, model), by_step, by_step]
        out_specs += [all_of(rows, model), all_of(rows, 1)] * 2
        out_shape += [shape(model, bf16), shape(4 * width, bf16), shape(4 * width, bf16)]
        out_shape += [shape(model, f32), shape(1, f32)] * 2
    flops = 2 * rows * model * (model + 8 * width)
    return pl.pallas_call(
        functools.partial(ffn_forward_kernel, keep),
        grid=(4,),
        in_specs=[
            pl.BlockSpec((rows, model), lambda i: (part, 0)),
            pl.BlockSpec((rows, model), lambda i: (part, 0)),
            all_of(model, model),
            *near_far(model, width),
            *near_far(width, model),
            pl.BlockSpec((1, width), lambda i: (0, i)),
            all_of(2, model),
            all_of(4, model),
        ],
        out_specs=out_specs,
        out_shape=out_shape,
        scratch_shapes=[pltpu.VMEM((rows, model), bf16), pltpu.VMEM((rows, model), f32)],
        compiler_params=pltpu.CompilerParams(vmem_limit_bytes=32 * MIB),
        cost_estimate=cost(15),
        name="ffn_forward",
    )(
        attended,
        inputs,
        w["out"],
        *w["up"],
        *w["down"],
        w["up_bias"],
        w["gains"],
        w["shifts"],
    )


def top_back_kernel(
    first_ref, came_ref, gy_ref, n_two_ref, s_two_ref, gain_ref, after_ref, second_ref, sums_ref
):
    gy = jnp.where(first_ref[0] == 1, came_ref[...], gy_ref[...]).astype(f32)
    after = norm_back(gy, gain_ref[1:2, :], n_two_ref[...], s_two_ref[...])
    low = after.astype(bf16)
    after_ref[...] = after
    second_ref[...] = low
    sums_ref[0:1, :] = jnp.sum(gy * n_two_ref[...], 0, keepdims=True)
    sums_ref[1:2, :] = jnp.sum(low.astype(f32), 0, keepdims=True)
    sums_ref[2:3, :] = jnp.sum(gy, 0, keepdims=True)
    sums_ref[3:8, :] = jnp.zeros((5, sums_ref.shape[1]), f32)


def top_back(w, saved, first_layer, came, grad_y):
    rows, model = grad_y.shape
    return pl.pallas_call(
        top_back_kernel,
        in_specs=[pl.BlockSpec(memory_space=pltpu.SMEM), *[IN_VMEM] * 5],
        out_specs=[IN_VMEM] * 3,
        out_shape=[
            jax.ShapeDtypeStruct((rows, model), f32),
            jax.ShapeDtypeStruct((rows, model), bf16),
            jax.ShapeDtypeStruct((8, model), f32),
        ],
        compiler_params=pltpu.CompilerParams(vmem_limit_bytes=16 * MIB),
        cost_estimate=cost(2),
        name="top_back",
    )(first_layer, came, grad_y, saved["n_two"], saved["s_two"], w["gains"])


def ffn_backward_kernel(deps, *refs):
    (
        after_ref,
        second_ref,
        slope_ref,
        n_one_ref,
        s_one_ref,
        out_ref,
        up_ref,
        up_far_ref,
        down_ref,
        down_far_ref,
        gain_ref,
    ) = refs[:11]
    hidden_ref, before_ref, branch_ref, att_ref, sums_ref, hidden_sums_ref, total = refs[11 + deps :]
    i = pl.program_id(0)

    def add_up(value):
        return jnp.sum(value, 0, keepdims=True)

    @pl.when(i == 0)
    def _():
        total[...] = after_ref[...]

    near = i < 2
    width = up_ref.shape[2]
    step = 256
    add = None
    for first in range(0, width, step):
        cols = slice(first, first + step)
        up = jnp.where(near, up_ref[0, :, cols], up_far_ref[0, :, cols])
        down = jnp.where(near, down_ref[0, cols, :], down_far_ref[0, cols, :])
        active = dotf(second_ref[...], down, NT)
        hidden = (active * slope_ref[:, cols].astype(f32)).astype(bf16)
        hidden_ref[:, cols] = hidden
        hidden_sums_ref[0, :, cols] = add_up(hidden.astype(f32))
        part = dotf(hidden, up, NT)
        add = part if add is None else add + part
    total[...] += add

    @pl.when(i == pl.num_programs(0) - 1)
    def _():
        normed = total[...]
        before = norm_back(normed, gain_ref[0:1, :], n_one_ref[...], s_one_ref[...])
        low = before.astype(bf16)
        before_ref[...] = before
        branch_ref[...] = low
        att_ref[...] = dotf(low, out_ref[...], NT).astype(bf16)
        sums_ref[0:1, :] = add_up(normed * n_one_ref[...])
        sums_ref[1:2, :] = add_up(low.astype(f32))
        sums_ref[2:3, :] = add_up(normed)
        sums_ref[3:8, :] = jnp.zeros((5, sums_ref.shape[1]), f32)


def ffn_backward(w, saved, after, second, deps=()):
    rows, model = after.shape
    width = w["up"][0].shape[2]
    all_of = lambda *shape: pl.BlockSpec(shape, lambda i: (0,) * len(shape))
    by_step = pl.BlockSpec((rows, width), lambda i: (0, i))
    by_block = pl.BlockSpec((1, 1, width), lambda i: (i, 0, 0))
    shape = lambda cols, kind: jax.ShapeDtypeStruct((rows, cols), kind)
    whole_rows = all_of(rows, model)
    return pl.pallas_call(
        functools.partial(ffn_backward_kernel, len(deps)),
        grid=(4,),
        in_specs=[
            whole_rows,
            whole_rows,
            by_step,
            whole_rows,
            all_of(rows, 1),
            all_of(model, model),
            *near_far(model, width),
            *near_far(width, model),
            all_of(2, model),
            *[pl.BlockSpec(memory_space=pl.ANY)] * len(deps),
        ],
        out_specs=[by_step, whole_rows, whole_rows, whole_rows, all_of(8, model), by_block],
        out_shape=[
            shape(4 * width, bf16),
            shape(model, f32),
            shape(model, bf16),
            shape(model, bf16),
            jax.ShapeDtypeStruct((8, model), f32),
            jax.ShapeDtypeStruct((4, 1, width), f32),
        ],
        scratch_shapes=[pltpu.VMEM((rows, model), f32)],
        compiler_params=pltpu.CompilerParams(vmem_limit_bytes=32 * MIB),
        cost_estimate=cost(15),
        name="ffn_backward",
    )(
        after,
        second,
        saved["slope"],
        saved["n_one"],
        saved["s_one"],
        w["out"],
        *w["up"],
        *w["down"],
        w["gains"],
        *deps,
    )


def weight_grad_kernel(l_ref, lo_ref, r_ref, ro_ref, o_ref):
    total = dotf(l_ref[...], r_ref[...], TN) + dotf(lo_ref[...], ro_ref[...], TN)
    o_ref[...] = total.astype(o_ref.dtype)


def weight_grad(left, left_far, right, right_far, kind, left_cols, right_cols):
    rows = left.shape[0]
    lf, ln, lw = left_cols
    rf, rn, rw = right_cols
    return pl.pallas_call(
        weight_grad_kernel,
        grid=(rn, ln),
        in_specs=[
            pl.BlockSpec((rows, lw), lambda j, i: (0, lf + i)),
            pl.BlockSpec((rows, lw), lambda j, i: (0, lf + i)),
            pl.BlockSpec((rows, rw), lambda j, i: (0, rf + j)),
            pl.BlockSpec((rows, rw), lambda j, i: (0, rf + j)),
        ],
        out_specs=pl.BlockSpec((lw, rw), lambda j, i: (i, j)),
        out_shape=jax.ShapeDtypeStruct((ln * lw, rn * rw), kind),
        compiler_params=pltpu.CompilerParams(vmem_limit_bytes=20 * MIB),
        cost_estimate=cost(4),
        name="weight_grad",
    )(left, left_far, right, right_far)


def split_grad_kernel(l_ref, lo_ref, r_ref, ro_ref, kept_ref, sent_ref):
    total = dotf(l_ref[...], r_ref[...], TN) + dotf(lo_ref[...], ro_ref[...], TN)
    half = total.shape[0] // 2
    kept_ref[...] = total[:half].astype(bf16)
    sent_ref[...] = total[half:].astype(bf16)


def split_grad(left, left_far, right, right_far, width):
    rows, model = right.shape
    count = left_far.shape[1] // width
    left_block = pl.BlockSpec((rows, width), lambda i: (0, i))
    right_block = pl.BlockSpec((rows, model), lambda i: (0, 0))
    made = pl.BlockSpec((width // 2, model), lambda i: (i, 0))
    shape = (count * width // 2, model)
    return pl.pallas_call(
        split_grad_kernel,
        grid=(count,),
        in_specs=[left_block, left_block, right_block, right_block],
        out_specs=[made, made],
        out_shape=[jax.ShapeDtypeStruct(shape, bf16)] * 2,
        compiler_params=pltpu.CompilerParams(vmem_limit_bytes=20 * MIB),
        cost_estimate=cost(4),
        name="split_grad",
    )(left, left_far, right, right_far)


def project_kernel(x_ref, near_ref, far_ref, bias_ref, *refs):
    inputs = x_ref[...]
    *refs, q_ref, kv_ref = refs
    if refs:
        keep_ref, a_ref, b_ref, x1_ref = refs
        inputs = jnp.where(keep_ref[0] == 1, inputs, jnp.concatenate([a_ref[...], b_ref[...]], 0))
        x1_ref[...] = inputs
    half = near_ref.shape[1]
    for which in range(3):
        weight = jnp.concatenate([near_ref[which], far_ref[which]], 0)
        bias = bias_ref[:, 2 * half * which : 2 * half * (which + 1)]
        made = (dotf(inputs, weight, NT) + bias).astype(bf16)
        if which == 0:
            q_ref[...] = made
        else:
            kv_ref[:, 2 * half * (which - 1) : 2 * half * which] = made


def project(inputs, near, far, bias, *instead):
    rows, model = inputs.shape
    shapes = [(rows, model)] * (2 if instead else 1) + [(rows, 2 * model)]
    extra = [pl.BlockSpec(memory_space=pltpu.SMEM), IN_VMEM, IN_VMEM] if instead else []
    return pl.pallas_call(
        project_kernel,
        in_specs=[IN_VMEM] * 4 + extra,
        out_specs=[IN_VMEM] * len(shapes),
        out_shape=[jax.ShapeDtypeStruct(shape, bf16) for shape in shapes],
        compiler_params=pltpu.CompilerParams(vmem_limit_bytes=20 * MIB),
        cost_estimate=cost(4),
        name="project",
    )(inputs, near, far, bias, *instead)


def input_back_kernel(*refs):
    q_ref, k_ref, k_came_ref, v_ref, v_came_ref, before_ref, *weights = refs[:8]
    near_ref, far_ref, grad_ref, low_ref, sums_ref = refs[8:]
    half = near_ref.shape[1] // 3
    total = before_ref[...]
    for which in range(3):
        if which == 0:
            mixed = q_ref[...]
        else:
            own, came = (k_ref, k_came_ref) if which == 1 else (v_ref, v_came_ref)
            other = jnp.concatenate([came[:, half:], came[:, :half]], 1)
            mixed = (own[...] + other.astype(f32)).astype(bf16)
        near_ref[:, half * which : half * which + half] = mixed[:, :half]
        far_ref[:, half * which : half * which + half] = mixed[:, half:]
        sums = jnp.sum(mixed.astype(f32), 0, keepdims=True)
        sums_ref[2 * which] = sums[:, :half]
        sums_ref[2 * which + 1] = sums[:, half:]
        weight = jnp.concatenate([weights[0][which], weights[1][which]], 0)
        total = total + dotf(mixed, weight)
    grad_ref[...] = total
    low_ref[...] = total.astype(bf16)


def input_back(q, k, k_came, v, v_came, before, near, far):
    rows, model = before.shape
    half = model // 2
    return pl.pallas_call(
        input_back_kernel,
        in_specs=[IN_VMEM] * 8,
        out_specs=[IN_VMEM] * 5,
        out_shape=[
            jax.ShapeDtypeStruct((rows, 3 * half), bf16),
            jax.ShapeDtypeStruct((rows, 3 * half), bf16),
            jax.ShapeDtypeStruct((rows, model), f32),
            jax.ShapeDtypeStruct((rows, model), bf16),
            jax.ShapeDtypeStruct((6, 1, half), f32),
        ],
        compiler_params=pltpu.CompilerParams(vmem_limit_bytes=24 * MIB),
        cost_estimate=cost(6),
        name="input_back",
    )(q, k, k_came, v, v_came, before, near, far)


def body(
    hidden,
    cotangent,
    pair_lengths,
    query_lengths,
    buckets,
    qkv_weight,
    qv_bias,
    out_weight,
    up_weight,
    ffn_bias,
    down_weight,
    norm_gains,
    vectors,
    bias_table,
):
    leading = lax.axis_index("section") == 0
    place = lax.axis_index("tensor")
    y, core = place // 2, place % 2
    plane = lax.axis_index("dp")
    planes = lax.axis_size("dp")
    odd = plane % 2
    local, model = hidden.shape[1], hidden.shape[2]
    total = 4 * local
    cols = qkv_weight.shape[3]
    width = up_weight.shape[2]
    heads = bias_table.shape[1]
    kinds = bias_table.shape[2] // 2
    near, far = slice(0, 2 * cols), slice(2 * cols, 4 * cols)

    def swap_z(value):
        return lax.ppermute(value, "dp", [(i, i ^ 1) for i in range(planes)])

    def mine(array):
        return lax.dynamic_index_in_dim(array, y, 0, keepdims=False)

    def theirs(array):
        return lax.dynamic_index_in_dim(array, 1 - y, 0, keepdims=False)

    def in_order(first, own, came, axis=0):
        return jnp.concatenate(
            [jnp.where(first, own, came), jnp.where(first, came, own)], axis
        )

    def own_half(block, axis=0):
        half = block.shape[axis] // 2
        return lax.dynamic_slice_in_dim(block, half * odd, half, axis)

    def edge_blocks(value):
        return value.reshape(2, local, model)

    def stage(work):
        shapes = jax.eval_shape(work)
        return lax.cond(
            pair_lengths[0] > 0,
            work,
            lambda: jax.tree.map(lambda leaf: jnp.zeros(leaf.shape, leaf.dtype), shapes),
        )

    qkv_own = qkv_weight[0].transpose(1, 2, 0)
    out_own, up_own, down_own = out_weight[0], up_weight[0], down_weight[0]
    small = jnp.concatenate([qv_bias[0].reshape(-1), ffn_bias[0], bias_table[0].reshape(-1)])

    x_sent, qkv_sent = theirs(hidden), own_half(qkv_own, 1)

    def first_stage():
        halves = own_half(out_own), own_half(up_own), own_half(down_own)
        return swap_y(small), swap_y(x_sent), swap_y(qkv_sent), halves

    small_y, x_came, qkv_y, (out_sent, up_sent, down_sent) = stage(first_stage)

    def gather_small():
        two = jnp.stack([small, small_y])
        four = jnp.concatenate([two, swap_c(two)])
        table = four[:, 2 * cols + width :].reshape(2 * heads, 4, kinds)
        table = jnp.pad(table, ((0, 0), (0, 4), (0, 0))).reshape(16 * heads, kinds)
        kind = jnp.pad(buckets, (1, 0))
        kind = lax.dynamic_slice_in_dim(kind, 256 * core, SPAN, 0)
        kind = jnp.stack([jnp.pad(kind, (s, 0), constant_values=-1)[:SPAN] for s in range(8)])
        kind = kind.reshape(1, 8 * SPAN)
        onehot = (kind == jnp.arange(kinds, dtype=jnp.int32)[:, None]).astype(bf16)
        window = jnp.dot(
            table, onehot[:, :SPAN].astype(f32), precision=lax.Precision.HIGHEST
        )
        qv_all = four[:, : 2 * cols].reshape(4, 2, cols)
        q_bias, v_bias = qv_all[:, 0].reshape(-1), qv_all[:, 1].reshape(-1)
        bias = jnp.concatenate([q_bias, jnp.zeros((model,), f32), v_bias])
        info = jnp.stack([mine(query_lengths), core, mine(pair_lengths)]).astype(jnp.int32)
        return (
            window,
            onehot,
            bias.reshape(1, 3 * model),
            four[:, 2 * cols : 2 * cols + width].reshape(1, 4 * width),
            info,
            in_order(y == 0, mine(hidden), x_came),
        )

    def second_stage():
        return swap_z(qkv_y), swap_y(out_sent), swap_y(up_sent), stage(gather_small)

    qkv_z, out_y, up_y, found = stage(second_stage)
    window, onehot, bias, up_bias, info, x0 = found
    w = dict(up_bias=up_bias, gains=norm_gains[0], shifts=vectors[0])

    def gather_qkv():
        near = jnp.concatenate([qkv_own, in_order(odd == 0, qkv_y, qkv_z, 1)], 1)
        far = swap_c(near)
        q, kv = project(x0, near, far, bias)
        return (near, far), q, kv, swap_c(kv)

    def third_stage():
        return stage(gather_qkv), swap_y(down_sent), swap_z(out_y), swap_z(up_y)

    (qkv, q, kv, kv_other), down_y, out_z, up_z = stage(third_stage)
    out = jnp.concatenate([out_own, in_order(odd == 0, out_y, out_z)], 0)
    up = jnp.stack([up_own, in_order(odd == 0, up_y, up_z)])

    def fourth_stage():
        found = stage(lambda: attend_forward(info, q, kv, kv_other, window)[0])
        return swap_z(down_y), swap_c(out), swap_c(up), found

    down_z, out_far, up_far, attended = stage(fourth_stage)
    down = jnp.stack([down_own, in_order(odd == 0, down_y, down_z)])
    down_far, w["out"] = stage(lambda: (swap_c(down), jnp.concatenate([out, out_far], 0)))
    w["down"] = down, down_far
    w["up"] = up, up_far

    def to_next(value):
        return lax.ppermute(value, "section", [(0, 1)])

    def to_last(value):
        return lax.ppermute(value, "section", [(1, 0)])

    middle = ffn_forward(w, attended, x0, False, 0, 2)[0]
    came_a, middle = stage(
        lambda: (to_next(middle), ffn_forward(w, attended, x0, False, 1, 2)[0])
    )
    came_b = stage(lambda: to_next(middle))

    first_layer = leading.astype(jnp.int32).reshape(1)

    def project_again():
        x1, q, kv = project(x0, *qkv, bias, first_layer, came_a, came_b)
        return x1, q, kv, swap_c(kv)

    x1, q, kv, kv_other = stage(project_again)
    top_sent = theirs(cotangent)

    def eighth_stage():
        attended, lse = attend_forward(info, q, kv, kv_other, window)
        return swap_y(top_sent), swap_c(x1), attended, lse

    top_came, inputs_far, attended, lse = stage(eighth_stage)
    grad_top = in_order(y == 0, mine(cotangent), top_came)
    result, normed_low, active, slope, n_one, s_one, n_two, s_two = ffn_forward(
        w, attended, x1, True
    )
    saved = dict(slope=slope, n_one=n_one, s_one=s_one, n_two=n_two, s_two=s_two)

    def dense_back(after, second):
        names = ("hidden", "before", "branch", "attended", "low_sums", "hidden_sums")
        return dict(zip(names, ffn_backward(w, saved, after, second)))

    def attention_back(grads, table, first, count):
        return attend_backward(
            info, q, kv, kv_other, grads["attended"], lse, window, table, first, count
        )

    after, second, top_sums = top_back(w, saved, jnp.zeros((1,), jnp.int32), grad_top, grad_top)

    def ninth_stage():
        return (
            swap_c(normed_low),
            swap_c(active[:, 2 * width :]),
            swap_c(attended[:, far]),
            dense_back(after, second),
        )

    normed_far, active_far, attended_far, grads = stage(ninth_stage)
    grad_q, grad_k, grad_v, k_far, v_far = attention_back(grads, False, 0, 6)

    def to_middle():
        k_came, v_came = swap_c(k_far), swap_c(v_far)
        found = input_back(grad_q, grad_k, k_came, grad_v, v_came, grads["before"], *qkv)
        return to_last(found[3])

    grad_middle = stage(to_middle)

    thirds = width // 3

    def down_grad(kind, first):
        return weight_grad(
            active, active_far, second, second_far, kind, (first, 3, thirds), (0, 1, model)
        )

    after, second, top_sums = top_back(w, saved, first_layer, grad_middle, grad_top)
    second_far = stage(lambda: swap_c(second))
    down_sent = down_grad(bf16, 3)

    def through_dense():
        grads = dense_back(after, second)
        hidden, branch = grads["hidden"], grads["branch"]
        hidden_far, branch_far = swap_c(hidden[:, 2 * width :]), swap_c(branch)
        return grads, hidden_far, branch_far, down_grad(bf16, 0)

    def send_dense(grads, hidden_far, branch_far):
        args = normed_low, normed_far, grads["hidden"], hidden_far
        sent = weight_grad(*args, bf16, (0, 3, thirds), (1, 1, width))
        branch = grads["branch"]
        return sent, split_grad(attended, attended_far, branch, branch_far, 2 * cols)

    def dense_and_sends():
        grads, hidden_far, branch_far, down_kept = through_dense()
        return grads, hidden_far, down_kept, send_dense(grads, hidden_far, branch_far)

    down_came, (grads, hidden_far, down_kept, sends) = stage(
        lambda: (swap_y(down_sent), stage(dense_and_sends))
    )
    up_sent, (out_kept, out_sent) = sends
    down = down_kept + down_came

    def through_attention():
        args = normed_low, normed_far, grads["hidden"], hidden_far
        kept = weight_grad(*args, bf16, (0, 3, thirds), (0, 1, width))
        return attention_back(grads, True, 0, 6), kept

    def through_input(q_grad, k_grad, v_grad, k_far, v_far):
        came = swap_c(k_far), swap_c(v_far)
        near, far, grad_input, grad_low, qv_sums = input_back(
            q_grad, k_grad, came[0], v_grad, came[1], grads["before"], *qkv
        )
        rest_kept, rest_sent = split_grad(near, swap_c(far), x1, inputs_far, 2 * cols)
        return rest_kept, rest_sent, grad_input, grad_low, qv_sums

    def after_down():
        up_came, out_came, (found, up_kept) = stage(
            lambda: (swap_y(up_sent), swap_y(out_sent), stage(through_attention))
        )
        *found, held = found
        found = stage(lambda: through_input(*found))
        return found, held, up_kept + up_came, out_kept + out_came

    def over_planes(value, beside):
        if planes != 4:
            return lax.psum(value, "dp"), stage(beside)
        rows = value.shape[0] // 2
        first, second = value[:rows], value[rows:]
        held, sent = jnp.where(odd == 0, first, second), jnp.where(odd == 0, second, first)
        came, found = stage(lambda: (swap_z(sent), stage(beside)))
        held = held + came
        far_planes = [(0, 2), (2, 0), (1, 3), (3, 1)]
        return held + stage(lambda: lax.ppermute(held, "dp", far_planes)), found

    def after_up():
        rest_kept, rest_sent, grad_input, grad_low, qv_sums = input_found

        def own_sums():
            sums = token_sums(held, qv_sums)
            sums = sums[:2] + swap_c(sums[2:])
            if planes == 4:
                sums = sums + swap_z(sums)
                sums = sums + lax.ppermute(sums, "dp", [(0, 2), (2, 0), (1, 3), (3, 1)])
            else:
                sums = lax.psum(sums, "dp")
            return sums, grad_down.astype(f32)[None]

        rest_came, (sums, down_out) = stage(
            lambda: (swap_y(rest_sent), stage(own_sums))
        )
        rest = rest_kept + rest_came
        grad_qkv, found = over_planes(
            rest, lambda: through_sums(sums, grad_input, grad_low)
        )
        return down_out, grad_qkv, found

    def through_sums(sums, grad_input, grad_low):
        edge_low = edge_blocks(jnp.where(leading, grad_low, result.astype(bf16)))
        edge_own = mine(edge_blocks(jnp.where(leading, grad_input, result)))
        edge_came = swap_y(theirs(edge_low)).astype(f32)
        edges = [jnp.where(y == 0, edge_own, edge_came), jnp.where(y == 0, edge_came, edge_own)]
        sums = sums[0] + swap_y(sums[1])
        at = heads * 2 * kinds
        vec_out = sums[at + 2 * cols + width :].reshape(1, 6, share)
        return (
            jnp.stack(edges)[None],
            sums[at : at + 2 * cols].reshape(1, 2, cols),
            sums[at + 2 * cols : at + 2 * cols + width].reshape(1, width),
            vec_out[:, :2],
            vec_out[:, 2:],
            sums[:at].reshape(1, heads, 2 * kinds),
        )

    share = model // 4

    def token_sums(held, qv_sums):
        wide = held.reshape(4 * heads, 2, 8 * SPAN)
        wide = jnp.stack([wide[:, 0] - wide[:, 1], wide[:, 1]], 1).reshape(8 * heads, 8 * SPAN)
        high = wide.astype(bf16)
        low = (wide - high.astype(f32)).astype(bf16)
        grad_table = dotf(high, onehot, NT) + dotf(low, onehot, NT)
        grad_table = grad_table.reshape(4, heads * 2 * kinds)
        q_sums, _, v_sums = qv_sums.reshape(3, 4, cols)
        grad_ffn = grads["hidden_sums"].reshape(4, width)
        low_sums = grads["low_sums"]
        rows = [low_sums[0], top_sums[0], low_sums[1], low_sums[2], top_sums[1], top_sums[2]]
        by_share = jnp.stack(rows).reshape(6, 4, share)
        by_share = by_share.transpose(1, 0, 2).reshape(4, 6 * share)
        by_share = jnp.stack(
            [lax.dynamic_index_in_dim(by_share, place ^ flip, 0, False) for flip in (0, 2, 1, 3)]
        )
        return jnp.concatenate([grad_table, q_sums, v_sums, grad_ffn, by_share], 1)

    grad_down, (input_found, held, *later) = stage(
        lambda: (lax.psum(down, "dp"), stage(after_down))
    )
    summed, (down_out, grad_qkv, found) = stage(lambda: (lax.psum(later, "dp"), stage(after_up)))

    def last_stage():
        back = swap_z(grad_qkv) if planes == 4 else grad_qkv
        return back, *[value.astype(f32)[None] for value in summed]

    back, up_out, out_out = stage(last_stage)
    if planes == 4:
        grad_qkv = in_order(odd == 0, grad_qkv, back)
    qkv_out = grad_qkv.astype(f32).reshape(1, 3, cols, model)
    edges, qv_out, ffn_out, gain_out, vec_out, table_out = found
    return (
        edges,
        qkv_out.transpose(0, 3, 1, 2),
        qv_out,
        out_out,
        up_out,
        ffn_out,
        down_out,
        gain_out,
        vec_out,
        table_out,
    )


def solution(mesh):
    return jax.shard_map(
        body,
        mesh=mesh,
        in_specs=(
            P("dp", "tensor", None),
            P("dp", "tensor", None),
            P("dp"),
            P("dp"),
            P(),
            P("section", None, None, "tensor"),
            P("section", None, "tensor"),
            P("section", "tensor", None),
            P("section", None, "tensor"),
            P("section", "tensor"),
            P("section", "tensor", None),
            P("section", None, None),
            P("section", None, None),
            P("section", "tensor", None),
        ),
        out_specs=(
            P("section", "dp", "tensor", None),
            P("section", None, None, "tensor"),
            P("section", None, "tensor"),
            P("section", "tensor", None),
            P("section", None, "tensor"),
            P("section", "tensor"),
            P("section", "tensor", None),
            P("section", None, "tensor"),
            P("section", None, "tensor"),
            P("section", "tensor", None),
        ),
        check_vma=False,
    )
```

profile of v0, /device:TPU:0, one launch (start us, length us, event | category | flops | bytes accessed | tf_op | source)
XLA Modules:
  0.0 484.8 jit_solution(16386317128512464818)
XLA Ops:
  11.2 21.9 %conditional.30 = (f32[1344]{0:T(1024)}, bf16[256,768]{1,0:T(8,128)(2,1)}, bf16[3,96,768]{2,1,0:T(8,128)(2,1)}, bf16[96,768]{1,0:T(8,128)(2,1)S(1)}, bf16[384,76...) conditional(s32[]{:T(128)} %bitcast.30, () %tuple.248, (f32[1344]{0:T(1024)S(1)}, bf16[2,256,768]{2,1,0:T(8,128)(2,1)}, ...), branch_computations={%region_0.1_spmd, %region_1.2_spmd} | conditional | flops 8 | bytes 7984428 | solution.py:800
  18.8 14.4 %collective-permute-done.22 = f32[1344]{0:T(1024)} collective-permute-done((f32[1344]{0:T(1024)S(1)}, f32[1344]{0:T(1024)}, u32[]{:S(2)}, u32[]{:S(2)}) %collective-permute-start.22) | collective-permute-done | bytes 5408 | tf_op jit(solution)/shard_map/cond/branch_1_fun/ppermute | solution.py:39
  33.2 17.9 %conditional.31 = (bf16[3,96,768]{2,1,0:T(8,128)(2,1)}, bf16[96,768]{1,0:T(8,128)(2,1)}, bf16[384,768]{1,0:T(8,128)(2,1)}, f32[48,1792]{1,0:T(8,128)}, bf16[32,1...) conditional(s32[]{:T(128)} %bitcast.30, () %tuple.247, ...), branch_computations={%region_2.3_spmd, %region_3.6_spmd} | conditional | flops 35931792 | bytes 13545034 | solution.py:800
  51.1 19.4 %conditional.32 = (bf16[3,384,768]{2,1,0:T(8,128)(2,1)}, bf16[3,384,768]{2,1,0:T(8,128)(2,1)}, bf16[512,768]{1,0:T(8,128)(2,1)}, bf16[512,1536]{1,0:T(8,128)(2,1...) conditional(s32[]{:T(128)} %bitcast.30, () %tuple.251, ...), branch_computations={%region_6.7_spmd, %region_7.10_spmd} | conditional | flops 5750787 | bytes 37586552 | solution.py:800
  54.7 15.8 %conditional.1 = (bf16[3,384,768]{2,1,0:T(8,128)(2,1)}, bf16[3,384,768]{2,1,0:T(8,128)(2,1)}, bf16[512,768]{1,0:T(8,128)(2,1)}, bf16[512,1536]{1,0:T(8,128)(2,1)}, bf16[512,1536]{1,0:T(8,128)(2,1)}) conditional(s32[]{:T(128)} %bitcast.7, () %tuple.144, (s32[]{:T(128)}, bf16[3,96,768]{2,1,0:T(8,128)(2,1)}, bf16[3,96,768]{2,1,0:T(8,128)(2,1)}, ...), branch_computations={%region_8.8_spmd, %region_9.9_spmd} | conditional | flops 5750785 | bytes 32277890 | solution.py:800
  74.4 20.0 %conditional.33 = (bf16[384,768]{1,0:T(8,128)(2,1)}, bf16[384,768]{1,0:T(8,128)(2,1)}, bf16[2,768,768]{2,1,0:T(8,128)(2,1)}, bf16[512,768]{1,0:T(8,128)(2,1)}) conditional(s32[]{:T(128)} %bitcast.30, () %tuple.254, (bf16[384,768]{1,0:T(8,128)(2,1)}, bf16[384,768]{1,0:T(8,128)(2,1)S(1)}, bf16[2,768,768]{2,1,0:T(8,128)(2,1)S(1)}, s32[2]{0:T(128)S(1)}, ...), branch_computations={%region_10.11_spmd, %region_11.14_spmd} | conditional | flops 2 | bytes 71955992 | solution.py:800
  76.3 18.1 %conditional.2 = (bf16[512,768]{1,0:T(8,128)(2,1)}) conditional(s32[]{:T(128)} %bitcast.8, () %tuple.148, (s32[3]{0:T(128)}, bf16[512,768]{1,0:T(8,128)(2,1)}, bf16[512,1536]{1,0:T(8,128)(2,1)}, bf16[512,1536]{1,0:T(8,128)(2,1)}, f32[48,1792]{1,0:T(8,128)}) %tuple.149), branch_computations={%region_12.12_spmd, %region_13.13_spmd} | conditional | bytes 57800008 | solution.py:800
  76.3 18.0 %attend_forward.2 = (bf16[512,768]{1,0:T(8,128)(2,1)}, f32[6,2,512]{2,1,0:T(2,128)}) custom-call(s32[3]{0:T(128)} %get-tuple-element.706.info_ref, bf16[512,768]{1,0:T(8,128)(2,1)} %get-tuple-element.707.q_ref, bf16[512,1536]{1,0:T(8,128)(2,1)} %get-tuple-element.708.k_ref.v_ref, bf16[512,1536]{1,0:T(8,128)(2,1)} %get-tuple-element.708.k_ref.v_ref, ...), custom_call_target="tpu_custom_call" | custom-call | bytes 57800000 | tf_op jit(solution)/shard_map/cond/branch_1_fun/cond/branch_1_fun/attend_forward/pallas_call | solution.py:202
  148.3 19.0 %conditional.38 = (bf16[256,768]{1,0:T(8,128)(2,1)}, bf16[512,768]{1,0:T(8,128)(2,1)}, bf16[512,768]{1,0:T(8,128)(2,1)}, f32[6,2,512]{2,1,0:T(2,128)S(1)}) conditional(s32[]{:T(128)} %bitcast.30, () %tuple.245, (bf16[2,256,768]{2,1,0:T(8,128)(2,1)S(1)}, s32[]{:T(128)}, bf16[512,768]{1,0:T(8,128)(2,1)}, s32[3]{0:T(128)}, ...), branch_computations={%region_22.23_spmd, %region_23.24_spmd} | conditional | bytes 63305140 | solution.py:800
  149.1 18.1 %attend_forward.3 = (bf16[512,768]{1,0:T(8,128)(2,1)}, f32[6,2,512]{2,1,0:T(2,128)S(1)}) custom-call(s32[3]{0:T(128)} %get-tuple-element.748.info_ref, bf16[512,768]{1,0:T(8,128)(2,1)S(1)} %get-tuple-element.749.q_ref, bf16[512,1536]{1,0:T(8,128)(2,1)} %get-tuple-element.750.k_ref.v_ref, bf16[512,1536]{1,0:T(8,128)(2,1)} %get-tuple-element.750.k_ref.v_ref, ...), custom_call_target="tpu_custom_call" | custom-call | bytes 57800000 | tf_op jit(solution)/shard_map/cond/branch_1_fun/attend_forward/pallas_call | solution.py:202
  169.3 17.9 %ffn_forward.5 = (f32[512,768]{1,0:T(8,128)}, bf16[512,768]{1,0:T(8,128)(2,1)}, bf16[512,3072]{1,0:T(8,128)(2,1)S(1)}, bf16[512,3072]{1,0:T(8,128)(2,1)}, f32[51...) custom-call(bf16[512,768]{1,0:T(8,128)(2,1)S(1)} %copy-done.12, ...), custom_call_target="tpu_custom_call" | custom-call | bytes 51000000 | tf_op jit(solution)/shard_map/ffn_forward/pallas_call | solution.py:453
  190.1 13.4 %conditional.39 = (bf16[512,768]{1,0:T(8,128)(2,1)}, bf16[512,1536]{1,0:T(8,128)(2,1)}, bf16[512,384]{1,0:T(8,128)(2,1)}, bf16[512,768]{1,0:T(8,128)(2,1)S(1)}, f32[512,768]{1,0:T(8,128)S(1)}) conditional(s32[]{:T(128)} %bitcast.30, () %tuple.262, (bf16[512,768]{1,0:T(8,128)(2,1)}, bf16[512,3072]{1,0:T(8,128)(2,1)S(1)}, ...), branch_computations={%region_24.25_spmd, %region_25.26_spmd} | conditional | bytes 65942368 | solution.py:800
  203.5 26.7 %attend_backward.3 = (bf16[512,768]{1,0:T(8,128)(2,1)}, f32[512,768]{1,0:T(8,128)}, f32[512,768]{1,0:T(8,128)}, bf16[512,768]{1,0:T(8,128)(2,1)}, bf16[512,768]{1,0:T(8,128)(2,1)}) custom-call(s32[3]{0:T(128)} %get-tuple-element.1175.refs_0_, bf16[512,768]{1,0:T(8,128)(2,1)S(1)} %get-tuple-element.1190.refs_1_, ...), custom_call_target="tpu_custom_call" | custom-call | bytes 102000000 | tf_op jit(solution)/shard_map/attend_backward/pallas_call | solution.py:311
  230.2 32.2 %conditional.40 = (bf16[512,768]{1,0:T(8,128)(2,1)}) conditional(s32[]{:T(128)} %bitcast.30, () %tuple.264, (bf16[512,768]{1,0:T(8,128)(2,1)}, bf16[512,768]{1,0:T(8,128)(2,1)}, bf16[512,768]{1,0:T(8,128)(2,1)}, f32[512,768]{1,0:T(8,128)}, f32[512,768]{1,0:T(8,128)}, /*index=5*/f32[512,768]{1,0:T(8,128)S(1)}, bf16[3,384,768]{2,1,0:T(8,128)(2,1)}, ...), branch_computations={%region_26.27_spmd, %region_27.28_spmd} | conditional | bytes 29837312 | solution.py:800
  241.7 20.7 %collective-permute-done.11 = bf16[512,768]{1,0:T(8,128)(2,1)} collective-permute-done((bf16[512,768]{1,0:T(8,128)(2,1)S(1)}, bf16[512,768]{1,0:T(8,128)(2,1)}, u32[]{:S(2)}, u32[]{:S(2)}) %collective-permute-start.11) | collective-permute-done | bytes 786464 | tf_op jit(solution)/shard_map/cond/branch_1_fun/ppermute | solution.py:878
  274.5 29.4 %conditional.42 = (bf16[768,768]{1,0:T(8,128)(2,1)}, bf16[512,768]{1,0:T(8,128)(2,1)}, f32[512,768]{1,0:T(8,128)}, bf16[512,3072]{1,0:T(8,128)(2,1)}, f32[4,1,76...) conditional(s32[]{:T(128)} %bitcast.30, () %tuple.244, ...), branch_computations={%region_30.31_spmd, %region_31.34_spmd} | conditional | flops 2 | bytes 121684896 | solution.py:800
  276.1 27.3 %conditional.3 = (bf16[512,768]{1,0:T(8,128)(2,1)}, f32[512,768]{1,0:T(8,128)}, bf16[512,3072]{1,0:T(8,128)(2,1)}, f32[4,1,768]{2,1,0:T(1,128)}, f32[8,768]{1,0:...) conditional(s32[]{:T(128)} %bitcast.10, () %tuple.164, ...), branch_computations={%region_32.32_spmd, %region_33.33_spmd} | conditional | bytes 116966016 | solution.py:800
  276.1 13.2 %ffn_backward.3 = (bf16[512,3072]{1,0:T(8,128)(2,1)}, f32[512,768]{1,0:T(8,128)}, bf16[512,768]{1,0:T(8,128)(2,1)S(1)}, bf16[512,768]{1,0:T(8,128)(2,1)}, f32[8,768]{1,0:T(8,128)}, /*index=5*/f32[4,1,768]{2,1,0:T(1,128)}) custom-call(f32[512,768]{1,0:T(8,128)} %get-tuple-element.780.refs_0_, bf16[512,768]{1,0:T(8,128)(2,1)S(1)} %get-tuple-element.781.refs_1_.r_ref, ...), custom_call_target="tpu_custom_call" | custom-call | bytes 51000000 | tf_op jit(solution)/shard_map/cond/branch_1_fun/cond/branch_1_fun/ffn_backward/pallas_call | solution.py:577
  303.8 62.8 %conditional.43 = (bf16[768,768]{1,0:T(8,128)(2,1)}, bf16[576,768]{1,0:T(8,128)(2,1)}, bf16[576,768]{1,0:T(8,128)(2,1)}, f32[512,768]{1,0:T(8,128)}, bf16[512,76...) conditional(s32[]{:T(128)} %bitcast.30, () %tuple.243, ...), branch_computations={%region_34.35_spmd, %region_35.45_spmd} | conditional | flops 1916934 | bytes 181549824 | solution.py:800
  306.9 59.7 %conditional.7 = (bf16[576,768]{1,0:T(8,128)(2,1)}, bf16[576,768]{1,0:T(8,128)(2,1)}, f32[512,768]{1,0:T(8,128)}, bf16[512,768]{1,0:T(8,128)(2,1)}, f32[6,1,384]...) conditional(s32[]{:T(128)} %bitcast.13, () %tuple.182, ...), branch_computations={%region_37.37_spmd, %region_38.44_spmd} | conditional | flops 737284 | bytes 170932704 | solution.py:800
  307.0 36.4 %conditional.5 = (bf16[768,768]{1,0:T(8,128)(2,1)}, bf16[192,768]{1,0:T(8,128)(2,1)}, bf16[512,768]{1,0:T(8,128)(2,1)}, f32[512,768]{1,0:T(8,128)}, f32[512,768]...) conditional(s32[]{:T(128)} %bitcast.12, () %tuple.178, ...), branch_computations={%region_39.38_spmd, %region_40.41_spmd} | conditional | flops 2 | bytes 121498552 | solution.py:800
  309.1 34.2 %conditional.4 = (bf16[512,768]{1,0:T(8,128)(2,1)}, f32[512,768]{1,0:T(8,128)}, f32[512,768]{1,0:T(8,128)}, bf16[512,768]{1,0:T(8,128)(2,1)}, bf16[512,768]{1,0:...) conditional(s32[]{:T(128)} %bitcast.11, () %tuple.172, (s32[3]{0:T(128)}, ...), branch_computations={%region_41.39_spmd, %region_42.40_spmd} | conditional | bytes 115600056 | solution.py:800
  313.9 29.5 %attend_backward.2 = (bf16[512,768]{1,0:T(8,128)(2,1)}, f32[512,768]{1,0:T(8,128)}, f32[512,768]{1,0:T(8,128)}, bf16[512,768]{1,0:T(8,128)(2,1)}, bf16[512,768]{...) custom-call(s32[3]{0:T(128)} %get-tuple-element.836.refs_0_, bf16[512,768]{1,0:T(8,128)(2,1)S(1)} %get-tuple-element.837.refs_1_, ...), custom_call_target="tpu_custom_call" | custom-call | bytes 102000000 | tf_op jit(solution)/shard_map/cond/branch_1_fun/cond/branch_1_fun/cond/branch_1_fun/cond/branch_1_fun/attend_backward/pallas_call | solution.py:311
  345.2 18.4 %conditional.6 = (bf16[576,768]{1,0:T(8,128)(2,1)}, bf16[576,768]{1,0:T(8,128)(2,1)}, f32[512,768]{1,0:T(8,128)}, bf16[512,768]{1,0:T(8,128)(2,1)}, f32[6,1,384]{2,1,0:T(1,128)}) conditional(s32[]{:T(128)} %bitcast.12, () %tuple.177, (bf16[512,768]{1,0:T(8,128)(2,1)}, bf16[512,768]{1,0:T(8,128)(2,1)}, bf16[512,768]{1,0:T(8,128)(2,1)}, ...), branch_computations={%region_43.42_spmd, %region_44.43_spmd} | conditional | bytes 45010208 | solution.py:800
  366.7 95.8 %conditional.44 = (bf16[768,768]{1,0:T(8,128)(2,1)}, bf16[192,768]{1,0:T(8,128)(2,1)}, f32[1,768,768]{2,1,0:T(8,128)}, bf16[288,768]{1,0:T(8,128)(2,1)}, f32[1,2...) conditional(s32[]{:T(128)} %bitcast.30, () %tuple.242, ...), branch_computations={%region_45.46_spmd, %region_46.61_spmd} | conditional | flops 51139400 | bytes 67364520 | solution.py:800
  367.6 94.1 %conditional.13 = (f32[1,768,768]{2,1,0:T(8,128)}, bf16[288,768]{1,0:T(8,128)(2,1)}, f32[1,2,256,768]{3,2,1,0:T(8,128)}, f32[1,2,192]{2,1,0:T(2,128)}, f32[1,768...) conditional(s32[]{:T(128)} %bitcast.27, () %tuple.205, ...), branch_computations={%region_49.49_spmd, %region_50.60_spmd} | conditional | flops 50402120 | bytes 58515352 | solution.py:800
  369.1 24.7 %conditional.10 = (bf16[576,768]{1,0:T(8,128)(2,1)}, f32[2,2496]{1,0:T(2,128)}, f32[1,768,768]{2,1,0:T(8,128)}) conditional(s32[]{:T(128)} %bitcast.26, () %tuple.199, (bf16[576,768]{1,0:T(8,128)(2,1)}, s32[2]{0:T(128)S(1)}, f32[6,2,2,8,1792]{4,3,2,1,0:T(8,128)}, bf16[32,14336]{1,0:T(8,128)(2,1)}, f32[6,1,384]{2,0,1:T(8,128)S(1)}, ...), branch_computations={%region_51.50_spmd, %region_52.53_spmd} | conditional | flops 46909824 | bytes 23513042 | solution.py:800
  370.2 23.6 %conditional.8 = (f32[2,2496]{1,0:T(2,128)}, f32[1,768,768]{2,1,0:T(8,128)}) conditional(s32[]{:T(128)} %bitcast.17, () %tuple.190, (f32[6,2,2,8,1792]{4,3,2,1,0:T(8,128)}, bf16[32,14336]{1,0:T(8,128)(2,1)}, f32[6,1,384]{2,0,1:T(8,128)S(1)}, f32[4,1,768]{2,0,1:T(4,128)S(1)}, f32[8,768]{1,0:T(8,128)}, /*index=5*/f32[8,768]{1,0:T(8,128)S(1)}, ...), branch_computations={%region_53.51_spmd, %region_54.52_spmd} | conditional | flops 46909824 | bytes 19973956 | solution.py:800
  395.7 19.6 %conditional.11 = (bf16[288,768]{1,0:T(8,128)(2,1)}, f32[1,2,256,768]{3,2,1,0:T(8,128)}, f32[1,2,192]{2,1,0:T(2,128)}, f32[1,768]{1,0:T(1,128)}, f32[1,2,192]{2,...) conditional(s32[]{:T(128)} %bitcast.26, () %tuple.201, (pred[]{:T(512)}, ...), branch_computations={%region_55.54_spmd, %region_56.57_spmd} | conditional | flops 2386378 | bytes 19377796 | solution.py:800
  396.8 18.6 %conditional.9 = (f32[1,2,256,768]{3,2,1,0:T(8,128)}, f32[1,2,192]{2,1,0:T(2,128)}, f32[1,768]{1,0:T(1,128)}, f32[1,2,192]{2,1,0:T(2,128)}, f32[1,4,192]{2,1,0:T(4,128)}, /*index=5*/f32[1,3,64]{2,1,0:T(4,128)}) conditional(s32[]{:T(128)} %bitcast.25, () %tuple.196, (s32[]{:T(128)}, pred[]{:T(512)}, f32[512,768]{1,0:T(8,128)}, ...), branch_computations={%region_57.55_spmd, %region_58.56_spmd} | conditional | flops 2165192 | bytes 16281060 | solution.py:800
  416.5 43.4 %conditional.12 = (bf16[288,768]{1,0:T(8,128)(2,1)}) conditional(s32[]{:T(128)} %bitcast.26, () %tuple.203, bf16[288,768]{1,0:T(8,128)(2,1)S(1)} %select_add_fusion), branch_computations={%region_59.58_spmd, %region_60.59_spmd} | conditional | bytes 1769520 | solution.py:800
  420.0 39.8 %collective-permute-done.21 = bf16[288,768]{1,0:T(8,128)(2,1)} collective-permute-done((bf16[288,768]{1,0:T(8,128)(2,1)S(1)}, bf16[288,768]{1,0:T(8,128)(2,1)}, u32[]{:S(2)}, u32[]{:S(2)}) %collective-permute-start.21) | collective-permute-done | bytes 442400 | tf_op jit(solution)/shard_map/cond/branch_1_fun/cond/branch_1_fun/cond/branch_1_fun/ppermute | solution.py:998
  (304 shorter events, 333.1 us)
Async XLA Ops:
  11.2 21.9 %collective-permute-start.24 = (bf16[3,96,768]{2,1,0:T(8,128)(2,1)S(1)}, bf16[3,96,768]{2,1,0:T(8,128)(2,1)}, u32[]{:S(2)}, u32[]{:S(2)}) collective-permute-start(bf16[3,96,768]{2,1,0:T(8,128)(2,1)S(1)} %get-tuple-element.651), channel_id=1, source_target_pairs={{0,2},{2,0},{1,3},{3,1},{4,6},{6,4},{5,7},{7,5},{8,10},{10,8},{9,1... | collective-permute-start | bytes 1327112 | tf_op jit(solution)/shard_map/cond/branch_1_fun/ppermute | solution.py:39
  15.4 17.8 %collective-permute-start.23 = (bf16[256,768]{1,0:T(8,128)(2,1)S(1)}, bf16[256,768]{1,0:T(8,128)(2,1)}, u32[]{:S(2)}, u32[]{:S(2)}) collective-permute-start(bf16[256,768]{1,0:T(8,128)(2,1)S(1)} %dynamic-slice_bitcast_fusion.2), channel_id=1, source_target_pairs={{0,2},{2,0},{1,3},{3,1},{4,6},{6,4},{5,7},{7,5},{8,10},{10,8},{9,1... | collective-permute-start | bytes 1179656 | tf_op jit(solution)/shard_map/cond/branch_1_fun/ppermute | solution.py:39
  15.4 17.7 %collective-permute-start.22 = (f32[1344]{0:T(1024)S(1)}, f32[1344]{0:T(1024)}, u32[]{:S(2)}, u32[]{:S(2)}) collective-permute-start(f32[1344]{0:T(1024)S(1)} %get-tuple-element.648), channel_id=1, source_target_pairs={{0,2},{2,0},{1,3},{3,1},{4,6},{6,4},{5,7},{7,5},{8,10},{10,8},{9,1... | collective-permute-start | bytes 16136 | tf_op jit(solution)/shard_map/cond/branch_1_fun/ppermute | solution.py:39
  33.2 17.9 %collective-permute-start.37 = (bf16[384,768]{1,0:T(8,128)(2,1)S(1)}, bf16[384,768]{1,0:T(8,128)(2,1)}, u32[]{:S(2)}, u32[]{:S(2)}) collective-permute-start(bf16[384,768]{1,0:T(8,128)(2,1)S(1)} %get-tuple-element.667), channel_id=1, source_target_pairs={{0,2},{2,0},{1,3},{3,1},{4,6},{6,4},{5,7},{7,5},{8,10},{10,8},{9,1... | collective-permute-start | bytes 1769480 | tf_op jit(solution)/shard_map/cond/branch_1_fun/ppermute | solution.py:39
  35.0 16.0 %collective-permute-start.35 = (bf16[3,96,768]{2,1,0:T(8,128)(2,1)}, bf16[3,96,768]{2,1,0:T(8,128)(2,1)}, u32[]{:S(2)}, u32[]{:S(2)}) collective-permute-start(bf16[3,96,768]{2,1,0:T(8,128)(2,1)} %get-tuple-element.665), channel_id=1, source_target_pairs={{0,4},{4,0},{8,12},{12,8},{1,5},{5,1},{9,13},{13,9},{2,6},{6,2},{1... | collective-permute-start | bytes 1327112 | tf_op jit(solution)/shard_map/cond/branch_1_fun/ppermute | solution.py:778
  36.6 14.5 %collective-permute-start.36 = (bf16[96,768]{1,0:T(8,128)(2,1)S(1)}, bf16[96,768]{1,0:T(8,128)(2,1)}, u32[]{:S(2)}, u32[]{:S(2)}) collective-permute-start(bf16[96,768]{1,0:T(8,128)(2,1)S(1)} %get-tuple-element.666), channel_id=1, source_target_pairs={{0,2},{2,0},{1,3},{3,1},{4,6},{6,4},{5,7},{7,5},{8,10},{10,8},{9,1... | collective-permute-start | bytes 442376 | tf_op jit(solution)/shard_map/cond/branch_1_fun/ppermute | solution.py:39
  51.1 19.3 %collective-permute-start.27 = (bf16[384,768]{1,0:T(8,128)(2,1)S(1)}, bf16[384,768]{1,0:T(8,128)(2,1)}, u32[]{:S(2)}, u32[]{:S(2)}) collective-permute-start(bf16[384,768]{1,0:T(8,128)(2,1)S(1)} %get-tuple-element.703), channel_id=1, source_target_pairs={{0,2},{2,0},{1,3},{3,1},{4,6},{6,4},{5,7},{7,5},{8,10},{10,8},{9,1... | collective-permute-start | bytes 1769480 | tf_op jit(solution)/shard_map/cond/branch_1_fun/ppermute | solution.py:39
  52.6 17.9 %collective-permute-start.29 = (bf16[384,768]{1,0:T(8,128)(2,1)}, bf16[384,768]{1,0:T(8,128)(2,1)}, u32[]{:S(2)}, u32[]{:S(2)}) collective-permute-start(bf16[384,768]{1,0:T(8,128)(2,1)} %get-tuple-element.705), channel_id=1, source_target_pairs={{0,4},{4,0},{8,12},{12,8},{1,5},{5,1},{9,13},{13,9},{2,6},{6,2},{1... | collective-permute-start | bytes 1769480 | tf_op jit(solution)/shard_map/cond/branch_1_fun/ppermute | solution.py:778
  54.2 16.3 %collective-permute-start.28 = (bf16[96,768]{1,0:T(8,128)(2,1)}, bf16[96,768]{1,0:T(8,128)(2,1)}, u32[]{:S(2)}, u32[]{:S(2)}) collective-permute-start(bf16[96,768]{1,0:T(8,128)(2,1)} %get-tuple-element.704), channel_id=1, source_target_pairs={{0,4},{4,0},{8,12},{12,8},{1,5},{5,1},{9,13},{13,9},{2,6},{6,2},{1... | collective-permute-start | bytes 442376 | tf_op jit(solution)/shard_map/cond/branch_1_fun/ppermute | solution.py:778
  74.4 20.0 %collective-permute-start.2 = (bf16[2,768,768]{2,1,0:T(8,128)(2,1)S(1)}, bf16[2,768,768]{2,1,0:T(8,128)(2,1)}, u32[]{:S(2)}, u32[]{:S(2)}) collective-permute-start(bf16[2,768,768]{2,1,0:T(8,128)(2,1)S(1)} %get-tuple-element.714), channel_id=1, source_target_pairs={{0,1},{1,0},{2,3},{3,2},{4,5},{5,4},{6,7},{7,6},{8,9},{9,8},{10,11... | collective-permute-start | bytes 7077896 | tf_op jit(solution)/shard_map/cond/branch_1_fun/ppermute | solution.py:43
  74.6 19.8 %collective-permute-start = (bf16[384,768]{1,0:T(8,128)(2,1)}, bf16[384,768]{1,0:T(8,128)(2,1)}, u32[]{:S(2)}, u32[]{:S(2)}) collective-permute-start(bf16[384,768]{1,0:T(8,128)(2,1)} %get-tuple-element.712), channel_id=1, source_target_pairs={{0,4},{4,0},{8,12},{12,8},{1,5},{5,1},{9,13},{13,9},{2,6},{6,2},{1... | collective-permute-start | bytes 1769480 | tf_op jit(solution)/shard_map/cond/branch_1_fun/ppermute | solution.py:778
  76.2 18.2 %collective-permute-start.1 = (bf16[384,768]{1,0:T(8,128)(2,1)S(1)}, bf16[384,768]{1,0:T(8,128)(2,1)}, u32[]{:S(2)}, u32[]{:S(2)}) collective-permute-start(bf16[384,768]{1,0:T(8,128)(2,1)S(1)} %get-tuple-element.713), channel_id=1, source_target_pairs={{0,1},{1,0},{2,3},{3,2},{4,5},{5,4},{6,7},{7,6},{8,9},{9,8},{10,11... | collective-permute-start | bytes 1769480 | tf_op jit(solution)/shard_map/cond/branch_1_fun/ppermute | solution.py:43
  114.0 13.1 %collective-permute-start.3 = (bf16[256,768]{1,0:T(8,128)(2,1)S(1)}, bf16[256,768]{1,0:T(8,128)(2,1)}, u32[]{:S(2)}, u32[]{:S(2)}) collective-permute-start(bf16[256,768]{1,0:T(8,128)(2,1)S(1)} %get-tuple-element.724), channel_id=1, source_target_pairs={{0,16},{1,17},{2,18},{3,19},{4,20},{5,21},{6,22},{7,23},{8,24},{9,... | collective-permute-start | bytes 1179656 | tf_op jit(solution)/shard_map/cond/branch_1_fun/ppermute | solution.py:875
  127.1 11.8 %collective-permute-start.4 = (bf16[256,768]{1,0:T(8,128)(2,1)S(1)}, bf16[256,768]{1,0:T(8,128)(2,1)}, u32[]{:S(2)}, u32[]{:S(2)}) collective-permute-start(bf16[256,768]{1,0:T(8,128)(2,1)S(1)} %param.19), channel_id=1, source_target_pairs={{0,16},{1,17},{2,18},{3,19},{4,20},{5,21},{6,22},{7,23},{8,24},{9,... | collective-permute-start | bytes 1179656 | tf_op jit(solution)/shard_map/cond/branch_1_fun/ppermute | solution.py:875
  148.3 18.8 %collective-permute-start.32 = (bf16[512,768]{1,0:T(8,128)(2,1)}, bf16[512,768]{1,0:T(8,128)(2,1)}, u32[]{:S(2)}, u32[]{:S(2)}) collective-permute-start(bf16[512,768]{1,0:T(8,128)(2,1)} %get-tuple-element.747), channel_id=1, source_target_pairs={{0,1},{1,0},{2,3},{3,2},{4,5},{5,4},{6,7},{7,6},{8,9},{9,8},{10,11... | collective-permute-start | bytes 2359304 | tf_op jit(solution)/shard_map/cond/branch_1_fun/ppermute | solution.py:43
  148.5 18.7 %collective-permute-start.31 = (bf16[256,768]{1,0:T(8,128)(2,1)S(1)}, bf16[256,768]{1,0:T(8,128)(2,1)}, u32[]{:S(2)}, u32[]{:S(2)}) collective-permute-start(bf16[256,768]{1,0:T(8,128)(2,1)S(1)} %dynamic-slice_bitcast_fusion.3), channel_id=1, source_target_pairs={{0,2},{2,0},{1,3},{3,1},{4,6},{6,4},{5,7},{7,5},{8,10},{10,8},{9,1... | collective-permute-start | bytes 1179656 | tf_op jit(solution)/shard_map/cond/branch_1_fun/ppermute | solution.py:39
  190.2 13.1 %collective-permute-start.7 = (bf16[512,1536]{1,0:T(8,128)(2,1)S(1)}, bf16[512,1536]{1,0:T(8,128)(2,1)}, u32[]{:S(2)}, u32[]{:S(2)}) collective-permute-start(bf16[512,1536]{1,0:T(8,128)(2,1)S(1)} %slice.142), channel_id=1, source_target_pairs={{0,1},{1,0},{2,3},{3,2},{4,5},{5,4},{6,7},{7,6},{8,9},{9,8},{10,11... | collective-permute-start | bytes 4718600 | tf_op jit(solution)/shard_map/cond/branch_1_fun/ppermute | solution.py:43
  190.3 13.0 %collective-permute-start.6 = (bf16[512,768]{1,0:T(8,128)(2,1)}, bf16[512,768]{1,0:T(8,128)(2,1)}, u32[]{:S(2)}, u32[]{:S(2)}) collective-permute-start(bf16[512,768]{1,0:T(8,128)(2,1)} %get-tuple-element.755), channel_id=1, source_target_pairs={{0,1},{1,0},{2,3},{3,2},{4,5},{5,4},{6,7},{7,6},{8,9},{9,8},{10,11... | collective-permute-start | bytes 2359304 | tf_op jit(solution)/shard_map/cond/branch_1_fun/ppermute | solution.py:43
  190.8 12.5 %collective-permute-start.8 = (bf16[512,384]{1,0:T(8,128)(2,1)S(1)}, bf16[512,384]{1,0:T(8,128)(2,1)}, u32[]{:S(2)}, u32[]{:S(2)}) collective-permute-start(bf16[512,384]{1,0:T(8,128)(2,1)S(1)} %slice.143), channel_id=1, source_target_pairs={{0,1},{1,0},{2,3},{3,2},{4,5},{5,4},{6,7},{7,6},{8,9},{9,8},{10,11... | collective-permute-start | bytes 1179656 | tf_op jit(solution)/shard_map/cond/branch_1_fun/ppermute | solution.py:43
  240.4 22.0 %collective-permute-start.11 = (bf16[512,768]{1,0:T(8,128)(2,1)S(1)}, bf16[512,768]{1,0:T(8,128)(2,1)}, u32[]{:S(2)}, u32[]{:S(2)}) collective-permute-start(bf16[512,768]{1,0:T(8,128)(2,1)S(1)} %get-tuple-element.779), channel_id=1, source_target_pairs={{16,0},{17,1},{18,2},{19,3},{20,4},{21,5},{22,6},{23,7},{24,8},{25... | collective-permute-start | bytes 2359304 | tf_op jit(solution)/shard_map/cond/branch_1_fun/ppermute | solution.py:878
  274.5 28.9 %collective-permute-start.15 = (bf16[768,768]{1,0:T(8,128)(2,1)}, bf16[768,768]{1,0:T(8,128)(2,1)}, u32[]{:S(2)}, u32[]{:S(2)}) collective-permute-start(bf16[768,768]{1,0:T(8,128)(2,1)} %get-tuple-element.806), channel_id=1, source_target_pairs={{0,2},{2,0},{1,3},{3,1},{4,6},{6,4},{5,7},{7,5},{8,10},{10,8},{9,1... | collective-permute-start | bytes 3538952 | tf_op jit(solution)/shard_map/cond/branch_1_fun/ppermute | solution.py:39
  291.1 7.6 %collective-permute-start.13 = (bf16[512,1536]{1,0:T(8,128)(2,1)S(1)}, bf16[512,1536]{1,0:T(8,128)(2,1)}, u32[]{:S(2)}, u32[]{:S(2)}) collective-permute-start(bf16[512,1536]{1,0:T(8,128)(2,1)S(1)} %slice.144), channel_id=1, source_target_pairs={{0,1},{1,0},{2,3},{3,2},{4,5},{5,4},{6,7},{7,6},{8,9},{9,8},{10,11... | collective-permute-start | bytes 4718600 | tf_op jit(solution)/shard_map/cond/branch_1_fun/cond/branch_1_fun/ppermute | solution.py:43
  303.9 62.8 %all-reduce.13.cloned.1.call-start = ((), (), s32[]{:S(2)}) async-start(), calls=%async_computation | async-start | bytes 2359296 | tf_op jit(solution)/shard_map/cond/branch_1_fun/psum | solution.py:1060
  307.0 36.4 %collective-permute-start.16 = (bf16[768,768]{1,0:T(8,128)(2,1)}, bf16[768,768]{1,0:T(8,128)(2,1)}, u32[]{:S(2)}, u32[]{:S(2)}) collective-permute-start(bf16[768,768]{1,0:T(8,128)(2,1)} %get-tuple-element.853), channel_id=1, source_target_pairs={{0,2},{2,0},{1,3},{3,1},{4,6},{6,4},{5,7},{7,5},{8,10},{10,8},{9,1... | collective-permute-start | bytes 3538952 | tf_op jit(solution)/shard_map/cond/branch_1_fun/cond/branch_1_fun/cond/branch_1_fun/ppermute | solution.py:39
  308.1 35.3 %collective-permute-start.17 = (bf16[192,768]{1,0:T(8,128)(2,1)}, bf16[192,768]{1,0:T(8,128)(2,1)}, u32[]{:S(2)}, u32[]{:S(2)}) collective-permute-start(bf16[192,768]{1,0:T(8,128)(2,1)} %get-tuple-element.854), channel_id=1, source_target_pairs={{0,2},{2,0},{1,3},{3,1},{4,6},{6,4},{5,7},{7,5},{8,10},{10,8},{9,1... | collective-permute-start | bytes 884744 | tf_op jit(solution)/shard_map/cond/branch_1_fun/cond/branch_1_fun/cond/branch_1_fun/ppermute | solution.py:39
  366.8 95.6 %all-reduce.15.cloned.1.call-start = ((), (), s32[]{:S(2)}) async-start(), calls=%async_computation.1 | async-start | bytes 2949120 | tf_op jit(solution)/shard_map/cond/branch_1_fun/psum | solution.py:1062
  369.1 24.7 %collective-permute-start.44 = (bf16[576,768]{1,0:T(8,128)(2,1)}, bf16[576,768]{1,0:T(8,128)(2,1)}, u32[]{:S(2)}, u32[]{:S(2)}) collective-permute-start(bf16[576,768]{1,0:T(8,128)(2,1)} %get-tuple-element.963), channel_id=1, source_target_pairs={{0,2},{2,0},{1,3},{3,1},{4,6},{6,4},{5,7},{7,5},{8,10},{10,8},{9,1... | collective-permute-start | bytes 2654216 | tf_op jit(solution)/shard_map/cond/branch_1_fun/cond/branch_1_fun/cond/branch_1_fun/ppermute | solution.py:39
  396.5 18.8 %collective-permute-start.40 = (bf16[288,768]{1,0:T(8,128)(2,1)}, bf16[288,768]{1,0:T(8,128)(2,1)}, u32[]{:S(2)}, u32[]{:S(2)}) collective-permute-start(bf16[288,768]{1,0:T(8,128)(2,1)} %broadcast_select_fusion.3), channel_id=1, source_target_pairs={{0,4},{4,0},{8,12},{12,8},{1,5},{5,1},{9,13},{13,9},{2,6},{6,2},{1... | collective-permute-start | bytes 1327112 | tf_op jit(solution)/shard_map/cond/branch_1_fun/cond/branch_1_fun/cond/branch_1_fun/ppermute | solution.py:778
  398.1 14.8 %collective-permute-start.38 = (bf16[256,768]{1,0:T(8,128)(2,1)S(1)}, bf16[256,768]{1,0:T(8,128)(2,1)S(1)}, u32[]{:S(2)}, u32[]{:S(2)}) collective-permute-start(bf16[256,768]{1,0:T(8,128)(2,1)S(1)} %dynamic-slice_bitcast_fusion.4), channel_id=1, source_target_pairs={{0,2},{2,0},{1,3},{3,1},{4,6},{6,4},{5,7},{7,5},{8,10},{10,8},{9,1... | collective-permute-start | bytes 1179656 | tf_op jit(solution)/shard_map/cond/branch_1_fun/cond/branch_1_fun/cond/branch_1_fun/cond/branch_1_fun/ppermute | solution.py:39
  400.3 9.2 %collective-permute-start.39 = (f32[2496]{0:T(1024)S(1)}, f32[2496]{0:T(1024)S(1)}, u32[]{:S(2)}, u32[]{:S(2)}) collective-permute-start(f32[2496]{0:T(1024)S(1)} %get-tuple-element.1302), channel_id=1, source_target_pairs={{0,2},{2,0},{1,3},{3,1},{4,6},{6,4},{5,7},{7,5},{8,10},{10,8},{9,1... | collective-permute-start | bytes 29960 | tf_op jit(solution)/shard_map/cond/branch_1_fun/cond/branch_1_fun/cond/branch_1_fun/cond/branch_1_fun/ppermute | solution.py:39
  416.5 43.3 %collective-permute-start.21 = (bf16[288,768]{1,0:T(8,128)(2,1)S(1)}, bf16[288,768]{1,0:T(8,128)(2,1)}, u32[]{:S(2)}, u32[]{:S(2)}) collective-permute-start(bf16[288,768]{1,0:T(8,128)(2,1)S(1)} %param.55), channel_id=1, source_target_pairs={{0,8},{8,0},{4,12},{12,4},{1,9},{9,1},{5,13},{13,5},{2,10},{10,2},... | collective-permute-start | bytes 1327112 | tf_op jit(solution)/shard_map/cond/branch_1_fun/cond/branch_1_fun/cond/branch_1_fun/ppermute | solution.py:998
  463.0 11.5 %collective-permute-start.33 = (bf16[288,768]{1,0:T(8,128)(2,1)}, bf16[288,768]{1,0:T(8,128)(2,1)}, u32[]{:S(2)}, u32[]{:S(2)}) collective-permute-start(bf16[288,768]{1,0:T(8,128)(2,1)} %get-tuple-element.1051), channel_id=1, source_target_pairs={{0,4},{4,0},{8,12},{12,8},{1,5},{5,1},{9,13},{13,9},{2,6},{6,2},{1... | collective-permute-start | bytes 1327112 | tf_op jit(solution)/shard_map/cond/branch_1_fun/ppermute | solution.py:778
  (50 other events, 359.2 us)
Sparse Core Ops, SparseCore 0:
  307.1 54.6 all-reduce.12
  370.1 90.9 all-reduce.14
where the time goes:
time: 495 us; the launch traced here: 485 us
  Pallas kernels  212 us (43%)
  waiting for transfers between devices  133 us (27%)
  other arithmetic  47.4 us (10%)
  starting transfers between devices  41.3 us (8%)
  local copies, waits for them, and re-layouts  28.6 us (6%)
  between operations  15.3 us (3%)
    pallas_call x2, Pallas kernels, attend_backward(): pl.pallas_call(functools.partial(backward_kernel, with_table), grid_spec=...  56.1 us
    ppermute x1, waiting for transfers between devices, over_planes(): return (held + stage(lambda: lax.ppermute(held, 'dp', far_planes)), found)  39.8 us
    pallas_call x3, Pallas kernels, ffn_forward(): pl.pallas_call(functools.partial(ffn_forward_kernel, keep), grid=(4,), in...  36.8 us
    pallas_call x2, Pallas kernels, attend_forward(): pl.pallas_call(forward_kernel, grid_spec=pltpu.PrefetchScalarGridSpec(num...  36.1 us
    ppermute x20, waiting for transfers between devices, swap_c(): return lax.ppermute(value, 'tensor', SWAP_C)  26.8 us
    pallas_call x2, Pallas kernels, ffn_backward(): pl.pallas_call(functools.partial(ffn_backward_kernel, len(deps)), grid=(4...  25.6 us
    ppermute x13, waiting for transfers between devices, swap_y(): return lax.ppermute(value, 'tensor', SWAP_Y)  22.7 us
    ppermute x1, waiting for transfers between devices, to_last(): return lax.ppermute(value, 'section', [(1, 0)])  20.7 us
  transfers between devices with their start and end apart: 47, of which 20 were waited for; matrix products, arithmetic and copies ran while one was open for 12% of the time, Pallas kernels for 28%

commit v1 on v0

--- a/solution.py
+++ b/solution.py
@@ -805,15 +805,16 @@
 
     qkv_own = qkv_weight[0].transpose(1, 2, 0)
     out_own, up_own, down_own = out_weight[0], up_weight[0], down_weight[0]
-    small = jnp.concatenate([qv_bias[0].reshape(-1), ffn_bias[0], bias_table[0].reshape(-1)])
-
     x_sent, qkv_sent = theirs(hidden), own_half(qkv_own, 1)
 
     def first_stage():
         halves = own_half(out_own), own_half(up_own), own_half(down_own)
-        return swap_y(small), swap_y(x_sent), swap_y(qkv_sent), halves
-
-    small_y, x_came, qkv_y, (out_sent, up_sent, down_sent) = stage(first_stage)
+        x_came, qkv_y = swap_y(x_sent), swap_y(qkv_sent)
+        small = [qv_bias[0].reshape(-1), ffn_bias[0], bias_table[0].reshape(-1)]
+        small = jnp.concatenate(small)
+        return small, swap_y(small), x_came, qkv_y, halves
+
+    small, small_y, x_came, qkv_y, (out_sent, up_sent, down_sent) = stage(first_stage)
 
     def gather_small():
         two = jnp.stack([small, small_y])

time: 495 us -> 492 us (level)
  transfers between devices with their start and end apart: 47 -> 47, of which waited for: 20 -> 20; matrix products, arithmetic and copies ran while one was open for 12% -> 13% of each run, Pallas kernels for 28% -> 28%
where the time goes in v1:
time: 492 us; the launch traced here: 483 us
  Pallas kernels  212 us (43%)
  waiting for transfers between devices  130 us (26%)
  other arithmetic  47.9 us (10%)
  starting transfers between devices  41.3 us (8%)
  local copies, waits for them, and re-layouts  29.2 us (6%)
  between operations  15.3 us (3%)
    pallas_call x2, Pallas kernels, attend_backward(): pl.pallas_call(functools.partial(backward_kernel, with_table), grid_spec=...  56.1 us
    ppermute x1, waiting for transfers between devices, over_planes(): return (held + stage(lambda: lax.ppermute(held, 'dp', far_planes)), found)  39.9 us
    pallas_call x3, Pallas kernels, ffn_forward(): pl.pallas_call(functools.partial(ffn_forward_kernel, keep), grid=(4,), in...  36.8 us
    pallas_call x2, Pallas kernels, attend_forward(): pl.pallas_call(forward_kernel, grid_spec=pltpu.PrefetchScalarGridSpec(num...  36.1 us
    ppermute x20, waiting for transfers between devices, swap_c(): return lax.ppermute(value, 'tensor', SWAP_C)  26.8 us
    pallas_call x2, Pallas kernels, ffn_backward(): pl.pallas_call(functools.partial(ffn_backward_kernel, len(deps)), grid=(4...  25.6 us
    ppermute x1, waiting for transfers between devices, to_last(): return lax.ppermute(value, 'section', [(1, 0)])  20.7 us
    pallas_call x4, Pallas kernels, weight_grad(): pl.pallas_call(weight_grad_kernel, grid=(rn, ln), in_specs=[pl.BlockSpec(...  19.5 us
  transfers between devices with their start and end apart: 47, of which 20 were waited for; matrix products, arithmetic and copies ran while one was open for 13% of the time, Pallas kernels for 28%

profile of v1, /device:TPU:0, one launch (start us, length us, event | category | flops | bytes accessed | tf_op | source)
XLA Modules:
  0.0 482.6 jit_solution(10976760495268720392)
XLA Ops:
  9.0 21.9 %conditional.30 = (f32[1344]{0:T(1024)}, f32[1344]{0:T(1024)}, bf16[256,768]{1,0:T(8,128)(2,1)}, bf16[3,96,768]{2,1,0:T(8,128)(2,1)}, bf16[96,768]{1,0:T(8,128)(...) conditional(s32[]{:T(128)} %bitcast.30, () %tuple.248, (f32[1,2,192]{2,1,0:T(2,128)}, ...), branch_computations={%region_0.1_spmd, %region_1.2_spmd} | conditional | flops 2696 | bytes 8007484 | solution.py:800
  30.9 17.9 %conditional.31 = (bf16[3,96,768]{2,1,0:T(8,128)(2,1)}, bf16[96,768]{1,0:T(8,128)(2,1)}, bf16[384,768]{1,0:T(8,128)(2,1)}, f32[48,1792]{1,0:T(8,128)}, bf16[32,1...) conditional(s32[]{:T(128)} %bitcast.30, () %tuple.247, ...), branch_computations={%region_2.3_spmd, %region_3.6_spmd} | conditional | flops 35931792 | bytes 13545034 | solution.py:800
  48.8 19.4 %conditional.32 = (bf16[3,384,768]{2,1,0:T(8,128)(2,1)}, bf16[3,384,768]{2,1,0:T(8,128)(2,1)}, bf16[512,768]{1,0:T(8,128)(2,1)}, bf16[512,1536]{1,0:T(8,128)(2,1...) conditional(s32[]{:T(128)} %bitcast.30, () %tuple.251, ...), branch_computations={%region_6.7_spmd, %region_7.10_spmd} | conditional | flops 5750787 | bytes 37586552 | solution.py:800
  52.4 15.8 %conditional.1 = (bf16[3,384,768]{2,1,0:T(8,128)(2,1)}, bf16[3,384,768]{2,1,0:T(8,128)(2,1)}, bf16[512,768]{1,0:T(8,128)(2,1)}, bf16[512,1536]{1,0:T(8,128)(2,1)}, bf16[512,1536]{1,0:T(8,128)(2,1)}) conditional(s32[]{:T(128)} %bitcast.7, () %tuple.144, (s32[]{:T(128)}, bf16[3,96,768]{2,1,0:T(8,128)(2,1)}, bf16[3,96,768]{2,1,0:T(8,128)(2,1)}, ...), branch_computations={%region_8.8_spmd, %region_9.9_spmd} | conditional | flops 5750785 | bytes 32277890 | solution.py:800
  72.1 20.0 %conditional.33 = (bf16[384,768]{1,0:T(8,128)(2,1)}, bf16[384,768]{1,0:T(8,128)(2,1)}, bf16[2,768,768]{2,1,0:T(8,128)(2,1)}, bf16[512,768]{1,0:T(8,128)(2,1)}) conditional(s32[]{:T(128)} %bitcast.30, () %tuple.254, (bf16[384,768]{1,0:T(8,128)(2,1)}, bf16[384,768]{1,0:T(8,128)(2,1)S(1)}, bf16[2,768,768]{2,1,0:T(8,128)(2,1)S(1)}, s32[2]{0:T(128)S(1)}, ...), branch_computations={%region_10.11_spmd, %region_11.14_spmd} | conditional | flops 2 | bytes 71955992 | solution.py:800
  74.0 18.1 %conditional.2 = (bf16[512,768]{1,0:T(8,128)(2,1)}) conditional(s32[]{:T(128)} %bitcast.8, () %tuple.148, (s32[3]{0:T(128)}, bf16[512,768]{1,0:T(8,128)(2,1)}, bf16[512,1536]{1,0:T(8,128)(2,1)}, bf16[512,1536]{1,0:T(8,128)(2,1)}, f32[48,1792]{1,0:T(8,128)}) %tuple.149), branch_computations={%region_12.12_spmd, %region_13.13_spmd} | conditional | bytes 57800008 | solution.py:800
  74.0 18.0 %attend_forward.2 = (bf16[512,768]{1,0:T(8,128)(2,1)}, f32[6,2,512]{2,1,0:T(2,128)}) custom-call(s32[3]{0:T(128)} %get-tuple-element.712.info_ref, bf16[512,768]{1,0:T(8,128)(2,1)} %get-tuple-element.713.q_ref, bf16[512,1536]{1,0:T(8,128)(2,1)} %get-tuple-element.714.k_ref.v_ref, bf16[512,1536]{1,0:T(8,128)(2,1)} %get-tuple-element.714.k_ref.v_ref, ...), custom_call_target="tpu_custom_call" | custom-call | bytes 57800000 | tf_op jit(solution)/shard_map/cond/branch_1_fun/cond/branch_1_fun/attend_forward/pallas_call | solution.py:202
  111.7 13.1 %conditional.35 = (bf16[256,768]{1,0:T(8,128)(2,1)}, bf16[256,768]{1,0:T(8,128)(2,1)S(1)}) conditional(s32[]{:T(128)} %bitcast.30, () %tuple.253, (bf16[256,768]{1,0:T(8,128)(2,1)S(1)}, bf16[512,768]{1,0:T(8,128)(2,1)}, bf16[512,768]{1,0:T(8,128)(2,1)}, bf16[768,768]{1,0:T(8,128)(2,1)S(1)}, bf16[2,768,768]{2,1,0:T(8,128)(2,1)S(1)}, ...), branch_computations={%region_16.17_spmd, %region_17.18_spmd} | conditional | bytes 52572920 | solution.py:800
  146.0 19.0 %conditional.38 = (bf16[256,768]{1,0:T(8,128)(2,1)}, bf16[512,768]{1,0:T(8,128)(2,1)}, bf16[512,768]{1,0:T(8,128)(2,1)}, f32[6,2,512]{2,1,0:T(2,128)S(1)}) conditional(s32[]{:T(128)} %bitcast.30, () %tuple.245, (bf16[2,256,768]{2,1,0:T(8,128)(2,1)S(1)}, s32[]{:T(128)}, bf16[512,768]{1,0:T(8,128)(2,1)}, s32[3]{0:T(128)}, ...), branch_computations={%region_22.23_spmd, %region_23.24_spmd} | conditional | bytes 63305140 | solution.py:800
  146.8 18.1 %attend_forward.3 = (bf16[512,768]{1,0:T(8,128)(2,1)}, f32[6,2,512]{2,1,0:T(2,128)S(1)}) custom-call(s32[3]{0:T(128)} %get-tuple-element.754.info_ref, bf16[512,768]{1,0:T(8,128)(2,1)S(1)} %get-tuple-element.755.q_ref, bf16[512,1536]{1,0:T(8,128)(2,1)} %get-tuple-element.756.k_ref.v_ref, bf16[512,1536]{1,0:T(8,128)(2,1)} %get-tuple-element.756.k_ref.v_ref, ...), custom_call_target="tpu_custom_call" | custom-call | bytes 57800000 | tf_op jit(solution)/shard_map/cond/branch_1_fun/attend_forward/pallas_call | solution.py:202
  167.0 17.9 %ffn_forward.5 = (f32[512,768]{1,0:T(8,128)}, bf16[512,768]{1,0:T(8,128)(2,1)}, bf16[512,3072]{1,0:T(8,128)(2,1)S(1)}, bf16[512,3072]{1,0:T(8,128)(2,1)}, f32[51...) custom-call(bf16[512,768]{1,0:T(8,128)(2,1)S(1)} %copy-done.12, ...), custom_call_target="tpu_custom_call" | custom-call | bytes 51000000 | tf_op jit(solution)/shard_map/ffn_forward/pallas_call | solution.py:453
  187.8 13.5 %conditional.39 = (bf16[512,768]{1,0:T(8,128)(2,1)}, bf16[512,1536]{1,0:T(8,128)(2,1)}, bf16[512,384]{1,0:T(8,128)(2,1)}, bf16[512,768]{1,0:T(8,128)(2,1)S(1)}, f32[512,768]{1,0:T(8,128)S(1)}) conditional(s32[]{:T(128)} %bitcast.30, () %tuple.262, (bf16[512,768]{1,0:T(8,128)(2,1)}, bf16[512,3072]{1,0:T(8,128)(2,1)S(1)}, ...), branch_computations={%region_24.25_spmd, %region_25.26_spmd} | conditional | bytes 65942368 | solution.py:800
  201.3 26.7 %attend_backward.3 = (bf16[512,768]{1,0:T(8,128)(2,1)}, f32[512,768]{1,0:T(8,128)}, f32[512,768]{1,0:T(8,128)}, bf16[512,768]{1,0:T(8,128)(2,1)}, bf16[512,768]{1,0:T(8,128)(2,1)}) custom-call(s32[3]{0:T(128)} %get-tuple-element.1183.refs_0_, bf16[512,768]{1,0:T(8,128)(2,1)S(1)} %get-tuple-element.1198.refs_1_, ...), custom_call_target="tpu_custom_call" | custom-call | bytes 102000000 | tf_op jit(solution)/shard_map/attend_backward/pallas_call | solution.py:311
  228.0 32.2 %conditional.40 = (bf16[512,768]{1,0:T(8,128)(2,1)}) conditional(s32[]{:T(128)} %bitcast.30, () %tuple.264, (bf16[512,768]{1,0:T(8,128)(2,1)}, bf16[512,768]{1,0:T(8,128)(2,1)}, bf16[512,768]{1,0:T(8,128)(2,1)}, f32[512,768]{1,0:T(8,128)}, f32[512,768]{1,0:T(8,128)}, /*index=5*/f32[512,768]{1,0:T(8,128)S(1)}, bf16[3,384,768]{2,1,0:T(8,128)(2,1)}, ...), branch_computations={%region_26.27_spmd, %region_27.28_spmd} | conditional | bytes 29837312 | solution.py:800
  239.4 20.7 %collective-permute-done.11 = bf16[512,768]{1,0:T(8,128)(2,1)} collective-permute-done((bf16[512,768]{1,0:T(8,128)(2,1)S(1)}, bf16[512,768]{1,0:T(8,128)(2,1)}, u32[]{:S(2)}, u32[]{:S(2)}) %collective-permute-start.11) | collective-permute-done | bytes 786464 | tf_op jit(solution)/shard_map/cond/branch_1_fun/ppermute | solution.py:879
  272.2 29.4 %conditional.42 = (bf16[768,768]{1,0:T(8,128)(2,1)}, bf16[512,768]{1,0:T(8,128)(2,1)}, f32[512,768]{1,0:T(8,128)}, bf16[512,3072]{1,0:T(8,128)(2,1)}, f32[4,1,76...) conditional(s32[]{:T(128)} %bitcast.30, () %tuple.244, ...), branch_computations={%region_30.31_spmd, %region_31.34_spmd} | conditional | flops 2 | bytes 121684896 | solution.py:800
  273.8 27.3 %conditional.3 = (bf16[512,768]{1,0:T(8,128)(2,1)}, f32[512,768]{1,0:T(8,128)}, bf16[512,3072]{1,0:T(8,128)(2,1)}, f32[4,1,768]{2,1,0:T(1,128)}, f32[8,768]{1,0:...) conditional(s32[]{:T(128)} %bitcast.10, () %tuple.164, ...), branch_computations={%region_32.32_spmd, %region_33.33_spmd} | conditional | bytes 116966016 | solution.py:800
  273.9 13.2 %ffn_backward.3 = (bf16[512,3072]{1,0:T(8,128)(2,1)}, f32[512,768]{1,0:T(8,128)}, bf16[512,768]{1,0:T(8,128)(2,1)S(1)}, bf16[512,768]{1,0:T(8,128)(2,1)}, f32[8,768]{1,0:T(8,128)}, /*index=5*/f32[4,1,768]{2,1,0:T(1,128)}) custom-call(f32[512,768]{1,0:T(8,128)} %get-tuple-element.786.refs_0_, bf16[512,768]{1,0:T(8,128)(2,1)S(1)} %get-tuple-element.787.refs_1_.r_ref, ...), custom_call_target="tpu_custom_call" | custom-call | bytes 51000000 | tf_op jit(solution)/shard_map/cond/branch_1_fun/cond/branch_1_fun/ffn_backward/pallas_call | solution.py:577
  301.6 62.8 %conditional.43 = (bf16[768,768]{1,0:T(8,128)(2,1)}, bf16[576,768]{1,0:T(8,128)(2,1)}, bf16[576,768]{1,0:T(8,128)(2,1)}, f32[512,768]{1,0:T(8,128)}, bf16[512,76...) conditional(s32[]{:T(128)} %bitcast.30, () %tuple.243, ...), branch_computations={%region_34.35_spmd, %region_35.45_spmd} | conditional | flops 1916934 | bytes 181549824 | solution.py:800
  304.7 59.7 %conditional.7 = (bf16[576,768]{1,0:T(8,128)(2,1)}, bf16[576,768]{1,0:T(8,128)(2,1)}, f32[512,768]{1,0:T(8,128)}, bf16[512,768]{1,0:T(8,128)(2,1)}, f32[6,1,384]...) conditional(s32[]{:T(128)} %bitcast.13, () %tuple.182, ...), branch_computations={%region_37.37_spmd, %region_38.44_spmd} | conditional | flops 737284 | bytes 170932704 | solution.py:800
  304.7 36.4 %conditional.5 = (bf16[768,768]{1,0:T(8,128)(2,1)}, bf16[192,768]{1,0:T(8,128)(2,1)}, bf16[512,768]{1,0:T(8,128)(2,1)}, f32[512,768]{1,0:T(8,128)}, f32[512,768]...) conditional(s32[]{:T(128)} %bitcast.12, () %tuple.178, ...), branch_computations={%region_39.38_spmd, %region_40.41_spmd} | conditional | flops 2 | bytes 121498552 | solution.py:800
  306.9 34.2 %conditional.4 = (bf16[512,768]{1,0:T(8,128)(2,1)}, f32[512,768]{1,0:T(8,128)}, f32[512,768]{1,0:T(8,128)}, bf16[512,768]{1,0:T(8,128)(2,1)}, bf16[512,768]{1,0:...) conditional(s32[]{:T(128)} %bitcast.11, () %tuple.172, (s32[3]{0:T(128)}, ...), branch_computations={%region_41.39_spmd, %region_42.40_spmd} | conditional | bytes 115600056 | solution.py:800
  311.6 29.5 %attend_backward.2 = (bf16[512,768]{1,0:T(8,128)(2,1)}, f32[512,768]{1,0:T(8,128)}, f32[512,768]{1,0:T(8,128)}, bf16[512,768]{1,0:T(8,128)(2,1)}, bf16[512,768]{...) custom-call(s32[3]{0:T(128)} %get-tuple-element.842.refs_0_, bf16[512,768]{1,0:T(8,128)(2,1)S(1)} %get-tuple-element.843.refs_1_, ...), custom_call_target="tpu_custom_call" | custom-call | bytes 102000000 | tf_op jit(solution)/shard_map/cond/branch_1_fun/cond/branch_1_fun/cond/branch_1_fun/cond/branch_1_fun/attend_backward/pallas_call | solution.py:311
  343.0 18.4 %conditional.6 = (bf16[576,768]{1,0:T(8,128)(2,1)}, bf16[576,768]{1,0:T(8,128)(2,1)}, f32[512,768]{1,0:T(8,128)}, bf16[512,768]{1,0:T(8,128)(2,1)}, f32[6,1,384]{2,1,0:T(1,128)}) conditional(s32[]{:T(128)} %bitcast.12, () %tuple.177, (bf16[512,768]{1,0:T(8,128)(2,1)}, bf16[512,768]{1,0:T(8,128)(2,1)}, bf16[512,768]{1,0:T(8,128)(2,1)}, ...), branch_computations={%region_43.42_spmd, %region_44.43_spmd} | conditional | bytes 45010208 | solution.py:800
  364.4 95.8 %conditional.44 = (bf16[768,768]{1,0:T(8,128)(2,1)}, bf16[192,768]{1,0:T(8,128)(2,1)}, f32[1,768,768]{2,1,0:T(8,128)}, bf16[288,768]{1,0:T(8,128)(2,1)}, f32[1,2...) conditional(s32[]{:T(128)} %bitcast.30, () %tuple.242, ...), branch_computations={%region_45.46_spmd, %region_46.61_spmd} | conditional | flops 51139400 | bytes 67364520 | solution.py:800
  365.3 94.1 %conditional.13 = (f32[1,768,768]{2,1,0:T(8,128)}, bf16[288,768]{1,0:T(8,128)(2,1)}, f32[1,2,256,768]{3,2,1,0:T(8,128)}, f32[1,2,192]{2,1,0:T(2,128)}, f32[1,768...) conditional(s32[]{:T(128)} %bitcast.27, () %tuple.205, ...), branch_computations={%region_49.49_spmd, %region_50.60_spmd} | conditional | flops 50402120 | bytes 58515352 | solution.py:800
  366.8 24.7 %conditional.10 = (bf16[576,768]{1,0:T(8,128)(2,1)}, f32[2,2496]{1,0:T(2,128)}, f32[1,768,768]{2,1,0:T(8,128)}) conditional(s32[]{:T(128)} %bitcast.26, () %tuple.199, (bf16[576,768]{1,0:T(8,128)(2,1)}, s32[2]{0:T(128)S(1)}, f32[6,2,2,8,1792]{4,3,2,1,0:T(8,128)}, bf16[32,14336]{1,0:T(8,128)(2,1)}, f32[6,1,384]{2,0,1:T(8,128)S(1)}, ...), branch_computations={%region_51.50_spmd, %region_52.53_spmd} | conditional | flops 46909824 | bytes 23513042 | solution.py:800
  367.9 23.6 %conditional.8 = (f32[2,2496]{1,0:T(2,128)}, f32[1,768,768]{2,1,0:T(8,128)}) conditional(s32[]{:T(128)} %bitcast.17, () %tuple.190, (f32[6,2,2,8,1792]{4,3,2,1,0:T(8,128)}, bf16[32,14336]{1,0:T(8,128)(2,1)}, f32[6,1,384]{2,0,1:T(8,128)S(1)}, f32[4,1,768]{2,0,1:T(4,128)S(1)}, f32[8,768]{1,0:T(8,128)}, /*index=5*/f32[8,768]{1,0:T(8,128)S(1)}, ...), branch_computations={%region_53.51_spmd, %region_54.52_spmd} | conditional | flops 46909824 | bytes 19973956 | solution.py:800
  393.5 19.6 %conditional.11 = (bf16[288,768]{1,0:T(8,128)(2,1)}, f32[1,2,256,768]{3,2,1,0:T(8,128)}, f32[1,2,192]{2,1,0:T(2,128)}, f32[1,768]{1,0:T(1,128)}, f32[1,2,192]{2,...) conditional(s32[]{:T(128)} %bitcast.26, () %tuple.201, (pred[]{:T(512)}, ...), branch_computations={%region_55.54_spmd, %region_56.57_spmd} | conditional | flops 2386378 | bytes 19377796 | solution.py:800
  394.5 18.6 %conditional.9 = (f32[1,2,256,768]{3,2,1,0:T(8,128)}, f32[1,2,192]{2,1,0:T(2,128)}, f32[1,768]{1,0:T(1,128)}, f32[1,2,192]{2,1,0:T(2,128)}, f32[1,4,192]{2,1,0:T(4,128)}, /*index=5*/f32[1,3,64]{2,1,0:T(4,128)}) conditional(s32[]{:T(128)} %bitcast.25, () %tuple.196, (s32[]{:T(128)}, pred[]{:T(512)}, f32[512,768]{1,0:T(8,128)}, ...), branch_computations={%region_57.55_spmd, %region_58.56_spmd} | conditional | flops 2165192 | bytes 16281060 | solution.py:800
  414.2 43.4 %conditional.12 = (bf16[288,768]{1,0:T(8,128)(2,1)}) conditional(s32[]{:T(128)} %bitcast.26, () %tuple.203, bf16[288,768]{1,0:T(8,128)(2,1)S(1)} %select_add_fusion), branch_computations={%region_59.58_spmd, %region_60.59_spmd} | conditional | bytes 1769520 | solution.py:800
  417.7 39.9 %collective-permute-done.21 = bf16[288,768]{1,0:T(8,128)(2,1)} collective-permute-done((bf16[288,768]{1,0:T(8,128)(2,1)S(1)}, bf16[288,768]{1,0:T(8,128)(2,1)}, u32[]{:S(2)}, u32[]{:S(2)}) %collective-permute-start.21) | collective-permute-done | bytes 442400 | tf_op jit(solution)/shard_map/cond/branch_1_fun/cond/branch_1_fun/cond/branch_1_fun/ppermute | solution.py:999
  (304 shorter events, 332.8 us)
Async XLA Ops:
  9.0 21.9 %collective-permute-start.33 = (bf16[3,96,768]{2,1,0:T(8,128)(2,1)S(1)}, bf16[3,96,768]{2,1,0:T(8,128)(2,1)}, u32[]{:S(2)}, u32[]{:S(2)}) collective-permute-start(bf16[3,96,768]{2,1,0:T(8,128)(2,1)S(1)} %get-tuple-element.657), channel_id=1, source_target_pairs={{0,2},{2,0},{1,3},{3,1},{4,6},{6,4},{5,7},{7,5},{8,10},{10,8},{9,1... | collective-permute-start | bytes 1327112 | tf_op jit(solution)/shard_map/cond/branch_1_fun/ppermute | solution.py:39
  13.1 17.8 %collective-permute-start.32 = (bf16[256,768]{1,0:T(8,128)(2,1)S(1)}, bf16[256,768]{1,0:T(8,128)(2,1)}, u32[]{:S(2)}, u32[]{:S(2)}) collective-permute-start(bf16[256,768]{1,0:T(8,128)(2,1)S(1)} %dynamic-slice_bitcast_fusion.3), channel_id=1, source_target_pairs={{0,2},{2,0},{1,3},{3,1},{4,6},{6,4},{5,7},{7,5},{8,10},{10,8},{9,1... | collective-permute-start | bytes 1179656 | tf_op jit(solution)/shard_map/cond/branch_1_fun/ppermute | solution.py:39
  16.0 14.9 %collective-permute-start.31 = (f32[1344]{0:T(1024)}, f32[1344]{0:T(1024)}, u32[]{:S(2)}, u32[]{:S(2)}) collective-permute-start(f32[1344]{0:T(1024)} %pad_maximum_fusion.5), channel_id=1, source_target_pairs={{0,2},{2,0},{1,3},{3,1},{4,6},{6,4},{5,7},{7,5},{8,10},{10,8},{9,1... | collective-permute-start | bytes 16136 | tf_op jit(solution)/shard_map/cond/branch_1_fun/ppermute | solution.py:39
  31.0 17.9 %collective-permute-start.37 = (bf16[384,768]{1,0:T(8,128)(2,1)S(1)}, bf16[384,768]{1,0:T(8,128)(2,1)}, u32[]{:S(2)}, u32[]{:S(2)}) collective-permute-start(bf16[384,768]{1,0:T(8,128)(2,1)S(1)} %get-tuple-element.673), channel_id=1, source_target_pairs={{0,2},{2,0},{1,3},{3,1},{4,6},{6,4},{5,7},{7,5},{8,10},{10,8},{9,1... | collective-permute-start | bytes 1769480 | tf_op jit(solution)/shard_map/cond/branch_1_fun/ppermute | solution.py:39
  32.8 16.0 %collective-permute-start.35 = (bf16[3,96,768]{2,1,0:T(8,128)(2,1)}, bf16[3,96,768]{2,1,0:T(8,128)(2,1)}, u32[]{:S(2)}, u32[]{:S(2)}) collective-permute-start(bf16[3,96,768]{2,1,0:T(8,128)(2,1)} %get-tuple-element.671), channel_id=1, source_target_pairs={{0,4},{4,0},{8,12},{12,8},{1,5},{5,1},{9,13},{13,9},{2,6},{6,2},{1... | collective-permute-start | bytes 1327112 | tf_op jit(solution)/shard_map/cond/branch_1_fun/ppermute | solution.py:778
  34.3 14.5 %collective-permute-start.36 = (bf16[96,768]{1,0:T(8,128)(2,1)S(1)}, bf16[96,768]{1,0:T(8,128)(2,1)}, u32[]{:S(2)}, u32[]{:S(2)}) collective-permute-start(bf16[96,768]{1,0:T(8,128)(2,1)S(1)} %get-tuple-element.672), channel_id=1, source_target_pairs={{0,2},{2,0},{1,3},{3,1},{4,6},{6,4},{5,7},{7,5},{8,10},{10,8},{9,1... | collective-permute-start | bytes 442376 | tf_op jit(solution)/shard_map/cond/branch_1_fun/ppermute | solution.py:39
  48.9 19.3 %collective-permute-start.24 = (bf16[384,768]{1,0:T(8,128)(2,1)S(1)}, bf16[384,768]{1,0:T(8,128)(2,1)}, u32[]{:S(2)}, u32[]{:S(2)}) collective-permute-start(bf16[384,768]{1,0:T(8,128)(2,1)S(1)} %get-tuple-element.709), channel_id=1, source_target_pairs={{0,2},{2,0},{1,3},{3,1},{4,6},{6,4},{5,7},{7,5},{8,10},{10,8},{9,1... | collective-permute-start | bytes 1769480 | tf_op jit(solution)/shard_map/cond/branch_1_fun/ppermute | solution.py:39
  50.3 17.9 %collective-permute-start.26 = (bf16[384,768]{1,0:T(8,128)(2,1)}, bf16[384,768]{1,0:T(8,128)(2,1)}, u32[]{:S(2)}, u32[]{:S(2)}) collective-permute-start(bf16[384,768]{1,0:T(8,128)(2,1)} %get-tuple-element.711), channel_id=1, source_target_pairs={{0,4},{4,0},{8,12},{12,8},{1,5},{5,1},{9,13},{13,9},{2,6},{6,2},{1... | collective-permute-start | bytes 1769480 | tf_op jit(solution)/shard_map/cond/branch_1_fun/ppermute | solution.py:778
  51.9 16.3 %collective-permute-start.25 = (bf16[96,768]{1,0:T(8,128)(2,1)}, bf16[96,768]{1,0:T(8,128)(2,1)}, u32[]{:S(2)}, u32[]{:S(2)}) collective-permute-start(bf16[96,768]{1,0:T(8,128)(2,1)} %get-tuple-element.710), channel_id=1, source_target_pairs={{0,4},{4,0},{8,12},{12,8},{1,5},{5,1},{9,13},{13,9},{2,6},{6,2},{1... | collective-permute-start | bytes 442376 | tf_op jit(solution)/shard_map/cond/branch_1_fun/ppermute | solution.py:778
  72.1 20.0 %collective-permute-start.2 = (bf16[2,768,768]{2,1,0:T(8,128)(2,1)S(1)}, bf16[2,768,768]{2,1,0:T(8,128)(2,1)}, u32[]{:S(2)}, u32[]{:S(2)}) collective-permute-start(bf16[2,768,768]{2,1,0:T(8,128)(2,1)S(1)} %get-tuple-element.720), channel_id=1, source_target_pairs={{0,1},{1,0},{2,3},{3,2},{4,5},{5,4},{6,7},{7,6},{8,9},{9,8},{10,11... | collective-permute-start | bytes 7077896 | tf_op jit(solution)/shard_map/cond/branch_1_fun/ppermute | solution.py:43
  72.3 19.8 %collective-permute-start = (bf16[384,768]{1,0:T(8,128)(2,1)}, bf16[384,768]{1,0:T(8,128)(2,1)}, u32[]{:S(2)}, u32[]{:S(2)}) collective-permute-start(bf16[384,768]{1,0:T(8,128)(2,1)} %get-tuple-element.718), channel_id=1, source_target_pairs={{0,4},{4,0},{8,12},{12,8},{1,5},{5,1},{9,13},{13,9},{2,6},{6,2},{1... | collective-permute-start | bytes 1769480 | tf_op jit(solution)/shard_map/cond/branch_1_fun/ppermute | solution.py:778
  73.9 18.2 %collective-permute-start.1 = (bf16[384,768]{1,0:T(8,128)(2,1)S(1)}, bf16[384,768]{1,0:T(8,128)(2,1)}, u32[]{:S(2)}, u32[]{:S(2)}) collective-permute-start(bf16[384,768]{1,0:T(8,128)(2,1)S(1)} %get-tuple-element.719), channel_id=1, source_target_pairs={{0,1},{1,0},{2,3},{3,2},{4,5},{5,4},{6,7},{7,6},{8,9},{9,8},{10,11... | collective-permute-start | bytes 1769480 | tf_op jit(solution)/shard_map/cond/branch_1_fun/ppermute | solution.py:43
  111.7 13.1 %collective-permute-start.3 = (bf16[256,768]{1,0:T(8,128)(2,1)S(1)}, bf16[256,768]{1,0:T(8,128)(2,1)}, u32[]{:S(2)}, u32[]{:S(2)}) collective-permute-start(bf16[256,768]{1,0:T(8,128)(2,1)S(1)} %get-tuple-element.730), channel_id=1, source_target_pairs={{0,16},{1,17},{2,18},{3,19},{4,20},{5,21},{6,22},{7,23},{8,24},{9,... | collective-permute-start | bytes 1179656 | tf_op jit(solution)/shard_map/cond/branch_1_fun/ppermute | solution.py:876
  124.8 11.8 %collective-permute-start.4 = (bf16[256,768]{1,0:T(8,128)(2,1)S(1)}, bf16[256,768]{1,0:T(8,128)(2,1)}, u32[]{:S(2)}, u32[]{:S(2)}) collective-permute-start(bf16[256,768]{1,0:T(8,128)(2,1)S(1)} %param.19), channel_id=1, source_target_pairs={{0,16},{1,17},{2,18},{3,19},{4,20},{5,21},{6,22},{7,23},{8,24},{9,... | collective-permute-start | bytes 1179656 | tf_op jit(solution)/shard_map/cond/branch_1_fun/ppermute | solution.py:876
  146.0 18.8 %collective-permute-start.29 = (bf16[512,768]{1,0:T(8,128)(2,1)}, bf16[512,768]{1,0:T(8,128)(2,1)}, u32[]{:S(2)}, u32[]{:S(2)}) collective-permute-start(bf16[512,768]{1,0:T(8,128)(2,1)} %get-tuple-element.753), channel_id=1, source_target_pairs={{0,1},{1,0},{2,3},{3,2},{4,5},{5,4},{6,7},{7,6},{8,9},{9,8},{10,11... | collective-permute-start | bytes 2359304 | tf_op jit(solution)/shard_map/cond/branch_1_fun/ppermute | solution.py:43
  146.2 18.7 %collective-permute-start.28 = (bf16[256,768]{1,0:T(8,128)(2,1)S(1)}, bf16[256,768]{1,0:T(8,128)(2,1)}, u32[]{:S(2)}, u32[]{:S(2)}) collective-permute-start(bf16[256,768]{1,0:T(8,128)(2,1)S(1)} %dynamic-slice_bitcast_fusion), channel_id=1, source_target_pairs={{0,2},{2,0},{1,3},{3,1},{4,6},{6,4},{5,7},{7,5},{8,10},{10,8},{9,1... | collective-permute-start | bytes 1179656 | tf_op jit(solution)/shard_map/cond/branch_1_fun/ppermute | solution.py:39
  187.9 13.1 %collective-permute-start.7 = (bf16[512,1536]{1,0:T(8,128)(2,1)S(1)}, bf16[512,1536]{1,0:T(8,128)(2,1)}, u32[]{:S(2)}, u32[]{:S(2)}) collective-permute-start(bf16[512,1536]{1,0:T(8,128)(2,1)S(1)} %slice.142), channel_id=1, source_target_pairs={{0,1},{1,0},{2,3},{3,2},{4,5},{5,4},{6,7},{7,6},{8,9},{9,8},{10,11... | collective-permute-start | bytes 4718600 | tf_op jit(solution)/shard_map/cond/branch_1_fun/ppermute | solution.py:43
  188.1 13.0 %collective-permute-start.6 = (bf16[512,768]{1,0:T(8,128)(2,1)}, bf16[512,768]{1,0:T(8,128)(2,1)}, u32[]{:S(2)}, u32[]{:S(2)}) collective-permute-start(bf16[512,768]{1,0:T(8,128)(2,1)} %get-tuple-element.761), channel_id=1, source_target_pairs={{0,1},{1,0},{2,3},{3,2},{4,5},{5,4},{6,7},{7,6},{8,9},{9,8},{10,11... | collective-permute-start | bytes 2359304 | tf_op jit(solution)/shard_map/cond/branch_1_fun/ppermute | solution.py:43
  188.5 12.5 %collective-permute-start.8 = (bf16[512,384]{1,0:T(8,128)(2,1)S(1)}, bf16[512,384]{1,0:T(8,128)(2,1)}, u32[]{:S(2)}, u32[]{:S(2)}) collective-permute-start(bf16[512,384]{1,0:T(8,128)(2,1)S(1)} %slice.143), channel_id=1, source_target_pairs={{0,1},{1,0},{2,3},{3,2},{4,5},{5,4},{6,7},{7,6},{8,9},{9,8},{10,11... | collective-permute-start | bytes 1179656 | tf_op jit(solution)/shard_map/cond/branch_1_fun/ppermute | solution.py:43
  238.1 22.0 %collective-permute-start.11 = (bf16[512,768]{1,0:T(8,128)(2,1)S(1)}, bf16[512,768]{1,0:T(8,128)(2,1)}, u32[]{:S(2)}, u32[]{:S(2)}) collective-permute-start(bf16[512,768]{1,0:T(8,128)(2,1)S(1)} %get-tuple-element.785), channel_id=1, source_target_pairs={{16,0},{17,1},{18,2},{19,3},{20,4},{21,5},{22,6},{23,7},{24,8},{25... | collective-permute-start | bytes 2359304 | tf_op jit(solution)/shard_map/cond/branch_1_fun/ppermute | solution.py:879
  272.2 28.9 %collective-permute-start.15 = (bf16[768,768]{1,0:T(8,128)(2,1)}, bf16[768,768]{1,0:T(8,128)(2,1)}, u32[]{:S(2)}, u32[]{:S(2)}) collective-permute-start(bf16[768,768]{1,0:T(8,128)(2,1)} %get-tuple-element.812), channel_id=1, source_target_pairs={{0,2},{2,0},{1,3},{3,1},{4,6},{6,4},{5,7},{7,5},{8,10},{10,8},{9,1... | collective-permute-start | bytes 3538952 | tf_op jit(solution)/shard_map/cond/branch_1_fun/ppermute | solution.py:39
  288.8 7.6 %collective-permute-start.13 = (bf16[512,1536]{1,0:T(8,128)(2,1)S(1)}, bf16[512,1536]{1,0:T(8,128)(2,1)}, u32[]{:S(2)}, u32[]{:S(2)}) collective-permute-start(bf16[512,1536]{1,0:T(8,128)(2,1)S(1)} %slice.144), channel_id=1, source_target_pairs={{0,1},{1,0},{2,3},{3,2},{4,5},{5,4},{6,7},{7,6},{8,9},{9,8},{10,11... | collective-permute-start | bytes 4718600 | tf_op jit(solution)/shard_map/cond/branch_1_fun/cond/branch_1_fun/ppermute | solution.py:43
  301.6 62.8 %all-reduce.13.cloned.1.call-start = ((), (), s32[]{:S(2)}) async-start(), calls=%async_computation | async-start | bytes 2359296 | tf_op jit(solution)/shard_map/cond/branch_1_fun/psum | solution.py:1061
  304.7 36.4 %collective-permute-start.16 = (bf16[768,768]{1,0:T(8,128)(2,1)}, bf16[768,768]{1,0:T(8,128)(2,1)}, u32[]{:S(2)}, u32[]{:S(2)}) collective-permute-start(bf16[768,768]{1,0:T(8,128)(2,1)} %get-tuple-element.859), channel_id=1, source_target_pairs={{0,2},{2,0},{1,3},{3,1},{4,6},{6,4},{5,7},{7,5},{8,10},{10,8},{9,1... | collective-permute-start | bytes 3538952 | tf_op jit(solution)/shard_map/cond/branch_1_fun/cond/branch_1_fun/cond/branch_1_fun/ppermute | solution.py:39
  305.8 35.3 %collective-permute-start.17 = (bf16[192,768]{1,0:T(8,128)(2,1)}, bf16[192,768]{1,0:T(8,128)(2,1)}, u32[]{:S(2)}, u32[]{:S(2)}) collective-permute-start(bf16[192,768]{1,0:T(8,128)(2,1)} %get-tuple-element.860), channel_id=1, source_target_pairs={{0,2},{2,0},{1,3},{3,1},{4,6},{6,4},{5,7},{7,5},{8,10},{10,8},{9,1... | collective-permute-start | bytes 884744 | tf_op jit(solution)/shard_map/cond/branch_1_fun/cond/branch_1_fun/cond/branch_1_fun/ppermute | solution.py:39
  364.6 95.6 %all-reduce.15.cloned.1.call-start = ((), (), s32[]{:S(2)}) async-start(), calls=%async_computation.1 | async-start | bytes 2949120 | tf_op jit(solution)/shard_map/cond/branch_1_fun/psum | solution.py:1063
  366.8 24.7 %collective-permute-start.44 = (bf16[576,768]{1,0:T(8,128)(2,1)}, bf16[576,768]{1,0:T(8,128)(2,1)}, u32[]{:S(2)}, u32[]{:S(2)}) collective-permute-start(bf16[576,768]{1,0:T(8,128)(2,1)} %get-tuple-element.969), channel_id=1, source_target_pairs={{0,2},{2,0},{1,3},{3,1},{4,6},{6,4},{5,7},{7,5},{8,10},{10,8},{9,1... | collective-permute-start | bytes 2654216 | tf_op jit(solution)/shard_map/cond/branch_1_fun/cond/branch_1_fun/cond/branch_1_fun/ppermute | solution.py:39
  394.3 18.8 %collective-permute-start.40 = (bf16[288,768]{1,0:T(8,128)(2,1)}, bf16[288,768]{1,0:T(8,128)(2,1)}, u32[]{:S(2)}, u32[]{:S(2)}) collective-permute-start(bf16[288,768]{1,0:T(8,128)(2,1)} %broadcast_select_fusion.3), channel_id=1, source_target_pairs={{0,4},{4,0},{8,12},{12,8},{1,5},{5,1},{9,13},{13,9},{2,6},{6,2},{1... | collective-permute-start | bytes 1327112 | tf_op jit(solution)/shard_map/cond/branch_1_fun/cond/branch_1_fun/cond/branch_1_fun/ppermute | solution.py:778
  395.8 14.8 %collective-permute-start.38 = (bf16[256,768]{1,0:T(8,128)(2,1)S(1)}, bf16[256,768]{1,0:T(8,128)(2,1)S(1)}, u32[]{:S(2)}, u32[]{:S(2)}) collective-permute-start(bf16[256,768]{1,0:T(8,128)(2,1)S(1)} %dynamic-slice_bitcast_fusion.4), channel_id=1, source_target_pairs={{0,2},{2,0},{1,3},{3,1},{4,6},{6,4},{5,7},{7,5},{8,10},{10,8},{9,1... | collective-permute-start | bytes 1179656 | tf_op jit(solution)/shard_map/cond/branch_1_fun/cond/branch_1_fun/cond/branch_1_fun/cond/branch_1_fun/ppermute | solution.py:39
  398.0 9.2 %collective-permute-start.39 = (f32[2496]{0:T(1024)S(1)}, f32[2496]{0:T(1024)S(1)}, u32[]{:S(2)}, u32[]{:S(2)}) collective-permute-start(f32[2496]{0:T(1024)S(1)} %get-tuple-element.1336), channel_id=1, source_target_pairs={{0,2},{2,0},{1,3},{3,1},{4,6},{6,4},{5,7},{7,5},{8,10},{10,8},{9,1... | collective-permute-start | bytes 29960 | tf_op jit(solution)/shard_map/cond/branch_1_fun/cond/branch_1_fun/cond/branch_1_fun/cond/branch_1_fun/ppermute | solution.py:39
  414.2 43.4 %collective-permute-start.21 = (bf16[288,768]{1,0:T(8,128)(2,1)S(1)}, bf16[288,768]{1,0:T(8,128)(2,1)}, u32[]{:S(2)}, u32[]{:S(2)}) collective-permute-start(bf16[288,768]{1,0:T(8,128)(2,1)S(1)} %param.55), channel_id=1, source_target_pairs={{0,8},{8,0},{4,12},{12,4},{1,9},{9,1},{5,13},{13,5},{2,10},{10,2},... | collective-permute-start | bytes 1327112 | tf_op jit(solution)/shard_map/cond/branch_1_fun/cond/branch_1_fun/cond/branch_1_fun/ppermute | solution.py:999
  460.7 11.5 %collective-permute-start.30 = (bf16[288,768]{1,0:T(8,128)(2,1)}, bf16[288,768]{1,0:T(8,128)(2,1)}, u32[]{:S(2)}, u32[]{:S(2)}) collective-permute-start(bf16[288,768]{1,0:T(8,128)(2,1)} %get-tuple-element.1057), channel_id=1, source_target_pairs={{0,4},{4,0},{8,12},{12,8},{1,5},{5,1},{9,13},{13,9},{2,6},{6,2},{1... | collective-permute-start | bytes 1327112 | tf_op jit(solution)/shard_map/cond/branch_1_fun/ppermute | solution.py:778
  (50 other events, 362.6 us)
Sparse Core Ops, SparseCore 0:
  304.8 54.6 all-reduce.12
  367.8 90.9 all-reduce.14
